TPU v7x, 256 devices: a whole 4x4x8 slice. The times are simulated.
256 devices in a mesh: dp: 4 (over x_hi, core), in: 4 (over y), out: 16 (over z, x_lo).
Axes of the slice: x: 4 (x_hi: 2, x_lo: 2; x = x_hi * 2 + x_lo), y: 4, z: 8, core: 2. Of those that a mesh axis runs over, the one named last changes fastest.
Arguments:
- inputs: bfloat16 [512, 8192], P(('dp', 'out'), 'in'), may hold values from -6 to 6
- context: bfloat16 [512, 4096], P('dp', 'out'), may hold values from -6 to 6
- gate_blocks: bfloat16 [4, 16, 240, 4096], P('in', 'out'), may hold values from -0.09375 to 0.09375
- gate_ids: int32 [4, 16, 240], P('in', 'out'), may hold values from 0 to 447, as said below
- gate_count: int32 [4, 16], P('in', 'out'), may hold values from 180 to 240
- up_blocks: bfloat16 [4, 16, 240, 4096], P('in', 'out'), may hold values from -0.09375 to 0.09375
- up_ids: int32 [4, 16, 240], P('in', 'out'), may hold values from 0 to 447, as said below
- up_count: int32 [4, 16], P('in', 'out'), may hold values from 180 to 240
- down_blocks: bfloat16 [16, 4, 240, 4096], P('out', 'in'), may hold values from -0.0625 to 0.0625
- down_ids: int32 [16, 4, 240], P('out', 'in'), may hold values from 0 to 447, as said below
- down_count: int32 [16, 4], P('out', 'in'), may hold values from 180 to 240
- heads_blocks: bfloat16 [16, 4, 68, 4096], P('out', 'in'), may hold values from -0.125 to 0.125
- heads_ids: int32 [16, 4, 68], P('out', 'in'), may hold values from 0 to 127, as said below
- heads_count: int32 [16, 4], P('out', 'in'), may hold values from 51 to 68
- cotangent: bfloat16 [512, 8192], P(('dp', 'out'), 'in'), may hold values from -6 to 6
Outputs:
- layer_output: bfloat16 [512, 8192], P(('dp', 'out'), 'in')
- input_grad: bfloat16 [512, 8192], P(('dp', 'out'), 'in')
- context_grad: bfloat16 [512, 4096], P('dp', 'out')
- gate_grads: bfloat16 [4, 16, 240, 4096], P('in', 'out', 'dp')
- up_grads: bfloat16 [4, 16, 240, 4096], P('in', 'out', 'dp')
- down_grads: bfloat16 [16, 4, 240, 4096], P('out', 'in', 'dp')
- heads_grads: bfloat16 [16, 4, 68, 4096], P('out', 'in', 'dp')
Inputs may be any that keep to these rules, and one draw needn't show every extreme that they name: `gate_ids`: entry r * 14 + c names block row r and block column c of a gate shard; all entries of one shard's list are distinct. `up_ids`: entry r * 14 + c names block row r and block column c of an up shard; all entries of one shard's list are distinct. `down_ids`: entry r * 32 + c names block row r (hidden units) and block column c (model width) of a down shard; all entries of one shard's list are distinct. `heads_ids`: entry r * 32 + c names block row r (attention features) and block column c (model width) of a shard; all entries of one shard's list are distinct.
All inputs are finite; a program needn't handle non-finite values.
Results may differ from a plain program's by a relative error of at most 0.039.
Values may be sent and summed in bfloat16 or wider, within the bound.
A program may use at most 128 MiB of HBM per device.

v0:
```python
import jax
import jax.numpy as jnp
from jax import lax
from jax.sharding import PartitionSpec as P

FF = 14336
BLOCK = 64


def as_sent(array):

    def short(part):
        return part.astype(jnp.bfloat16) if part.dtype == jnp.float32 else part

    return jax.tree.map(short, array)


def place_local(blocks, slot_ids, counts, block_rows, block_cols):
    slot_total = slot_ids.shape[-1]
    flat_ids = slot_ids.reshape(slot_total)
    present = jnp.arange(slot_total, dtype=jnp.int32) < counts.reshape(())
    pieces = blocks.reshape(slot_total, BLOCK * BLOCK)
    pieces = jnp.where(present[:, None], pieces, jnp.zeros_like(pieces))
    filled = jnp.zeros((block_rows * block_cols, BLOCK * BLOCK), blocks.dtype)
    filled = filled.at[flat_ids].set(pieces)
    filled = filled.reshape(block_rows, block_cols, BLOCK, BLOCK).transpose(0, 2, 1, 3)
    return filled.reshape(block_rows * BLOCK, block_cols * BLOCK)


def pick_local(matrix, slot_ids, counts, block_cols):
    slot_total = slot_ids.shape[-1]
    flat_ids = slot_ids.reshape(slot_total)
    present = jnp.arange(slot_total, dtype=jnp.int32) < counts.reshape(())
    block_rows = matrix.shape[0] // BLOCK
    shaped = matrix.reshape(block_rows, BLOCK, block_cols, BLOCK)
    pieces = shaped[flat_ids // block_cols, :, flat_ids % block_cols, :].reshape(
        slot_total, BLOCK * BLOCK
    )
    return jnp.where(present[:, None], pieces, jnp.zeros_like(pieces)).astype(jnp.float32)


def product_nt(left_side, right_side):
    return lax.dot_general(
        left_side, right_side, (((1,), (1,)), ((), ())), preferred_element_type=jnp.float32
    )


def product_tn(left_side, right_side):
    return lax.dot_general(
        left_side, right_side, (((0,), (0,)), ((), ())), preferred_element_type=jnp.float32
    )


def rounded_tn(left_side, right_side):
    return product_tn(left_side, right_side).astype(jnp.bfloat16)


def local(
    inputs,
    context,
    gate_blocks,
    gate_ids,
    gate_count,
    up_blocks,
    up_ids,
    up_count,
    down_blocks,
    down_ids,
    down_count,
    heads_blocks,
    heads_ids,
    heads_count,
    cotangent,
):
    width_blocks = inputs.shape[1] // BLOCK
    hidden_blocks = FF // BLOCK // lax.axis_size("out")
    context_blocks = context.shape[1] // BLOCK
    gate_matrix = place_local(gate_blocks, gate_ids, gate_count, width_blocks, hidden_blocks)
    up_matrix = place_local(up_blocks, up_ids, up_count, width_blocks, hidden_blocks)
    down_matrix = place_local(down_blocks, down_ids, down_count, hidden_blocks, width_blocks)
    heads_matrix = place_local(heads_blocks, heads_ids, heads_count, context_blocks, width_blocks)
    own_rows = inputs.shape[0]

    def rows_over_out(local_rows):
        return lax.all_gather(local_rows, "out", axis=0, tiled=True)

    def sum_over_out(term_fn):
        return lax.psum_scatter(
            term_fn(jnp.int32(0), own_rows * lax.axis_size("out")).astype(jnp.bfloat16),
            "out",
            scatter_dimension=0,
            tiled=True,
        ).astype(jnp.float32)

    def total_over_in(partials):
        return jax.tree.map(
            lambda part: part.astype(jnp.float32), lax.psum(as_sent(partials), "in")
        )

    def attention_term(first_row, row_count):
        return jnp.dot(context, heads_matrix, preferred_element_type=jnp.float32)

    residual = (inputs.astype(jnp.float32) + sum_over_out(attention_term)).astype(jnp.bfloat16)
    residual_rows = rows_over_out(residual)
    gate_sum, up_sum = total_over_in(
        (
            jnp.dot(residual_rows, gate_matrix, preferred_element_type=jnp.float32),
            jnp.dot(residual_rows, up_matrix, preferred_element_type=jnp.float32),
        )
    )
    sigmoid_gate = jax.nn.sigmoid(gate_sum)
    hidden = (gate_sum * sigmoid_gate * up_sum).astype(jnp.bfloat16)

    def down_term(first_row, row_count):
        return jnp.dot(hidden, down_matrix, preferred_element_type=jnp.float32)

    layer_output = (residual.astype(jnp.float32) + sum_over_out(down_term)).astype(jnp.bfloat16)
    cotangent_rows = rows_over_out(cotangent)
    (hidden_grad,) = total_over_in((product_nt(cotangent_rows, down_matrix),))
    gate_delta = (
        hidden_grad * up_sum * sigmoid_gate * (1.0 + gate_sum * (1.0 - sigmoid_gate))
    ).astype(jnp.bfloat16)
    up_delta = (hidden_grad * gate_sum * sigmoid_gate).astype(jnp.bfloat16)

    def back_term(first_row, row_count):
        return product_nt(gate_delta, gate_matrix) + product_nt(up_delta, up_matrix)

    input_grad = (cotangent.astype(jnp.float32) + sum_over_out(back_term)).astype(jnp.bfloat16)
    input_rows = rows_over_out(input_grad)
    (context_sum,) = total_over_in((product_nt(input_rows, heads_matrix),))
    context_grad = context_sum.astype(jnp.bfloat16)
    block_terms = (
        pick_local(rounded_tn(residual_rows, gate_delta), gate_ids, gate_count, hidden_blocks),
        pick_local(rounded_tn(residual_rows, up_delta), up_ids, up_count, hidden_blocks),
        pick_local(rounded_tn(hidden, cotangent_rows), down_ids, down_count, width_blocks),
        pick_local(rounded_tn(context, input_rows), heads_ids, heads_count, width_blocks),
    )
    summed = (
        lax.psum_scatter(
            block_terms[0].astype(jnp.bfloat16), "dp", scatter_dimension=0, tiled=True
        ).astype(jnp.float32),
        lax.psum_scatter(
            block_terms[1].astype(jnp.bfloat16), "dp", scatter_dimension=0, tiled=True
        ).astype(jnp.float32),
        lax.psum_scatter(
            block_terms[2].astype(jnp.bfloat16), "dp", scatter_dimension=0, tiled=True
        ).astype(jnp.float32),
        lax.psum_scatter(
            block_terms[3].astype(jnp.bfloat16), "dp", scatter_dimension=0, tiled=True
        ).astype(jnp.float32),
    )
    gate_share, up_share, down_share, heads_share = [
        item_sum.astype(jnp.bfloat16) for item_sum in summed
    ]
    gate_grads = gate_share.reshape(1, 1, -1, BLOCK * BLOCK)
    up_grads = up_share.reshape(1, 1, -1, BLOCK * BLOCK)
    down_grads = down_share.reshape(1, 1, -1, BLOCK * BLOCK)
    heads_grads = heads_share.reshape(1, 1, -1, BLOCK * BLOCK)
    return (layer_output, input_grad, context_grad, gate_grads, up_grads, down_grads, heads_grads)


def solution(mesh):
    placed = (
        P(("dp", "out"), "in"),
        P("dp", "out"),
        P("in", "out", None, None),
        P("in", "out", None),
        P("in", "out"),
        P("in", "out", None, None),
        P("in", "out", None),
        P("in", "out"),
        P("out", "in", None, None),
        P("out", "in", None),
        P("out", "in"),
        P("out", "in", None, None),
        P("out", "in", None),
        P("out", "in"),
        P(("dp", "out"), "in"),
    )
    return jax.shard_map(
        local,
        mesh=mesh,
        in_specs=placed,
        out_specs=(
            P(("dp", "out"), "in"),
            P(("dp", "out"), "in"),
            P("dp", "out"),
            P("in", "out", "dp", None),
            P("in", "out", "dp", None),
            P("out", "in", "dp", None),
            P("out", "in", "dp", None),
        ),
        check_vma=False,
    )
```

profile of v0, /device:TPU:2, one launch (start us, length us, event | category | flops | bytes accessed | tf_op | source)
XLA Modules:
  0.0 662.3 jit_solution(17148839790820274188)
XLA Ops:
  15.9 3.4 reshape.632
  20.8 4.0 copy.114
  25.5 4.0 copy.111
  30.2 4.0 copy.108
  35.1 3.2 bitcast_select_fusion.3
  41.3 4.1 copy.115
  45.5 6.9 %scatter_custom_fusion.3 = bf16[448,4096]{1,0:T(8,128)(2,1)} fusion(s32[240]{0:T(256)S(1)} %bitcast.153, bf16[240,4096]{1,0:T(8,128)(2,1)} %copy.115, bf16[]{:T(256)} %constant.69.clone.1), kind=kCustom, calls=%fused_computation.24 | custom fusion | bytes 3670528 | tf_op jit(solution)/shard_map/scatter | solution.py:25
  52.4 11.1 %reshape.646 = bf16[14,32,64,64]{3,2,1,0:T(8,128)(2,1)} reshape(bf16[448,4096]{1,0:T(8,128)(2,1)} %scatter_custom_fusion.3) | data formatting | bytes 7340032 | tf_op jit(solution)/shard_map/reshape | solution.py:26
  63.4 12.1 %copy.116 = bf16[14,64,32,64]{3,2,1,0:T(8,128)(2,1)} copy(bf16[14,64,32,64]{3,1,2,0:T(8,128)(2,1)} %bitcast.146) | data formatting | bytes 7340032 | tf_op jit(solution)/shard_map/transpose | solution.py:26
  75.5 11.1 %reshape.647 = bf16[896,2048]{1,0:T(8,128)(2,1)} reshape(bf16[14,64,32,64]{3,2,1,0:T(8,128)(2,1)} %copy.116) | data formatting | bytes 7340032 | tf_op jit(solution)/shard_map/reshape | solution.py:27
  86.5 4.1 copy.112
  90.7 7.1 %scatter_custom_fusion.2 = bf16[448,4096]{1,0:T(8,128)(2,1)} fusion(s32[240]{0:T(256)S(1)} %bitcast.155, bf16[240,4096]{1,0:T(8,128)(2,1)} %copy.112, bf16[]{:T(256)} %constant.69.clone.1), kind=kCustom, calls=%fused_computation.26 | custom fusion | bytes 3670528 | tf_op jit(solution)/shard_map/scatter | solution.py:25
  97.8 11.1 %reshape.641 = bf16[32,14,64,64]{3,2,1,0:T(8,128)(2,1)} reshape(bf16[448,4096]{1,0:T(8,128)(2,1)} %scatter_custom_fusion.2) | data formatting | bytes 7340032 | tf_op jit(solution)/shard_map/reshape | solution.py:26
  108.9 11.3 %copy.113 = bf16[32,64,14,64]{1,0,3,2:T(8,128)(2,1)} copy(bf16[32,64,14,64]{3,1,2,0:T(8,128)(2,1)} %bitcast.147) | data formatting | bytes 7340032 | tf_op jit(solution)/shard_map/transpose | solution.py:26
  120.2 11.1 %reshape.642 = bf16[2048,896]{0,1:T(8,128)(2,1)} reshape(bf16[32,64,14,64]{1,0,3,2:T(8,128)(2,1)} %copy.113) | data formatting | bytes 7340032 | tf_op jit(solution)/shard_map/reshape | solution.py:27
  131.2 4.1 copy.109
  135.4 6.7 %scatter_custom_fusion.1 = bf16[448,4096]{1,0:T(8,128)(2,1)} fusion(s32[240]{0:T(256)S(1)} %bitcast.154, bf16[240,4096]{1,0:T(8,128)(2,1)} %copy.109, bf16[]{:T(256)} %constant.69.clone.1), kind=kCustom, calls=%fused_computation.28 | custom fusion | bytes 3670528 | tf_op jit(solution)/shard_map/scatter | solution.py:25
  142.1 11.1 %reshape.636 = bf16[32,14,64,64]{3,2,1,0:T(8,128)(2,1)} reshape(bf16[448,4096]{1,0:T(8,128)(2,1)} %scatter_custom_fusion.1) | data formatting | bytes 7340032 | tf_op jit(solution)/shard_map/reshape | solution.py:26
  153.1 11.3 %copy.110 = bf16[32,64,14,64]{1,0,3,2:T(8,128)(2,1)} copy(bf16[32,64,14,64]{3,1,2,0:T(8,128)(2,1)} %bitcast.148) | data formatting | bytes 7340032 | tf_op jit(solution)/shard_map/transpose | solution.py:26
  164.4 11.1 %reshape.637 = bf16[2048,896]{0,1:T(8,128)(2,1)} reshape(bf16[32,64,14,64]{1,0,3,2:T(8,128)(2,1)} %copy.110) | data formatting | bytes 7340032 | tf_op jit(solution)/shard_map/reshape | solution.py:27
  175.5 36.5 %all_gather.10 = bf16[128,2048]{1,0:T(8,128)(2,1)S(1)} all-gather(bf16[8,2048]{1,0:T(8,128)(2,1)S(1)} %copy-done.9), channel_id=1, replica_groups=mesh['dp'=4,'in'=4,'out'=16] {'out'}, dimensions={0}, use_global_device_ids=true | all-gather | bytes 557056 | tf_op jit(solution)/shard_map/all_gather | solution.py:85
  212.0 4.0 fusion.10
  217.0 36.2 %all_gather.9 = bf16[128,2048]{1,0:T(8,128)(2,1)S(1)} all-gather(bf16[8,2048]{1,0:T(8,128)(2,1)S(1)} %add_convert_fusion.2), channel_id=1, replica_groups=mesh['dp'=4,'in'=4,'out'=16] {'out'}, dimensions={0}, use_global_device_ids=true | all-gather | bytes 557056 | tf_op jit(solution)/shard_map/all_gather | solution.py:85
  253.2 4.0 convolution_convert_fusion.7
  259.3 46.9 %all-reduce.13.cloned.1.call-done = (bf16[128,896]{1,0:T(8,128)(2,1)}, bf16[128,896]{1,0:T(8,128)(2,1)}, bf16[128,896]{1,0:T(8,128)(2,1)}) async-done(((bf16[128,896]{1,0:T(8,128)(2,1)}, bf16[128,896]{1,0:T(8,128)(2,1)}, bf16[128,896]{1,0:T(8,128)(2,1)}), (bf16[128,896]{1,0:T(8,128)(2,1)}, bf16[128,896]{1,0:T(8,128)(2,1)}, bf16[128,896]{1,0:T(8,128)(2,1)})) %all-reduce.13.cloned.1.call-update) | async-done | bytes 688144 | tf_op jit(solution)/shard_map/psum | solution.py:97
  306.1 3.9 convolution_convert_fusion.4
  317.6 11.6 %reshape.716 = bf16[32,64,14,64]{3,2,1,0:T(8,128)(2,1)} reshape(bf16[2048,896]{1,0:T(8,128)(2,1)} %convolution_convert_fusion.2) | data formatting | bytes 7340032 | tf_op jit(solution)/shard_map/reshape | solution.py:35
  329.2 8.3 %copy.121 = bf16[32,64,14,64]{3,1,2,0:T(8,128)(2,1)} copy(bf16[32,64,14,64]{3,2,1,0:T(8,128)(2,1)} %reshape.716) | data formatting | bytes 7340032 | tf_op jit(solution)/shard_map/reshape | solution.py:35
  337.5 7.0 %gather_fusion = bf16[240,64,64]{2,1,0:T(8,128)(2,1)} fusion(bf16[32,64,14,64]{3,1,2,0:T(8,128)(2,1)} %copy.121, s32[240]{0:T(256)S(1)} %bitcast.151), kind=kCustom, calls=%fused_computation | custom fusion | bytes 3934080 | tf_op jit(solution)/shard_map/gather | solution.py:36
  344.4 5.8 copy.122
  356.2 11.6 %reshape.717 = bf16[32,64,14,64]{3,2,1,0:T(8,128)(2,1)} reshape(bf16[2048,896]{1,0:T(8,128)(2,1)} %convolution_convert_fusion.1) | data formatting | bytes 7340032 | tf_op jit(solution)/shard_map/reshape | solution.py:35
  367.7 8.3 %copy.124 = bf16[32,64,14,64]{3,1,2,0:T(8,128)(2,1)} copy(bf16[32,64,14,64]{3,2,1,0:T(8,128)(2,1)} %reshape.717) | data formatting | bytes 7340032 | tf_op jit(solution)/shard_map/reshape | solution.py:35
  376.0 7.0 %gather_fusion.1 = bf16[240,64,64]{2,1,0:T(8,128)(2,1)} fusion(bf16[32,64,14,64]{3,1,2,0:T(8,128)(2,1)} %copy.124, s32[240]{0:T(256)S(1)} %bitcast.150), kind=kCustom, calls=%fused_computation.1 | custom fusion | bytes 3934080 | tf_op jit(solution)/shard_map/gather | solution.py:36
  383.0 5.7 copy.125
  388.7 3.1 bitcast_select_fusion.1
  392.1 3.1 convolution_convert_fusion
  395.2 11.3 %reshape.654 = bf16[14,64,32,64]{3,2,1,0:T(8,128)(2,1)} reshape(bf16[896,2048]{1,0:T(8,128)(2,1)} %convolution_convert_fusion) | data formatting | bytes 7340032 | tf_op jit(solution)/shard_map/reshape | solution.py:35
  406.5 9.1 %copy.126 = bf16[14,64,32,64]{3,1,2,0:T(8,128)(2,1)} copy(bf16[14,64,32,64]{3,2,1,0:T(8,128)(2,1)} %reshape.654) | data formatting | bytes 7340032 | tf_op jit(solution)/shard_map/reshape | solution.py:35
  415.6 6.9 %gather_fusion.2 = bf16[240,64,64]{2,1,0:T(8,128)(2,1)} fusion(bf16[14,64,32,64]{3,1,2,0:T(8,128)(2,1)} %copy.126, s32[240]{0:T(256)S(1)} %bitcast.149), kind=kCustom, calls=%fused_computation.2 | custom fusion | bytes 3934080 | tf_op jit(solution)/shard_map/gather | solution.py:36
  422.5 5.7 copy.127
  428.3 3.1 bitcast_select_fusion
  434.7 34.0 %all_gather.11 = bf16[128,2048]{1,0:T(8,128)(2,1)S(1)} all-gather(bf16[8,2048]{1,0:T(8,128)(2,1)S(1)} %add_convert_fusion), channel_id=1, replica_groups=mesh['dp'=4,'in'=4,'out'=16] {'out'}, dimensions={0}, use_global_device_ids=true | all-gather | bytes 557056 | tf_op jit(solution)/shard_map/all_gather | solution.py:85
  471.0 4.3 copy.128
  475.3 3.5 gather_fusion.3
  479.8 21.0 %fusion = bf16[24,4096]{1,0:T(8,128)(2,1)S(1)} fusion(bf16[68,4096]{1,0:T(8,128)(2,1)S(1)} %broadcast_select_fusion), kind=kCustom, calls=%all-reduce-scatter | all-reduce-scatter fusion | flops 393217 | bytes 754688
  506.2 98.2 %all-reduce.15.cloned.1.call-done = (bf16[240,4096]{0,1:T(8,128)(2,1)}, bf16[240,4096]{0,1:T(8,128)(2,1)}, bf16[240,4096]{0,1:T(8,128)(2,1)}) async-done(((bf16[240,4096]{0,1:T(8,128)(2,1)}, bf16[240,4096]{0,1:T(8,128)(2,1)}, bf16[240,4096]{0,1:T(8,128)(2,1)}), (bf16[240,4096]{0,1:T(8,128)(2,1)}, bf16[240,4096]{0,1:T(8,128)(2,1)}, bf16[240,4096]{0,1:T(8,128)(2,1)})) %all-reduce.15.cloned.1.call-update) | async-done | bytes 5898256
  604.4 3.1 dynamic-slice_bitcast_fusion
  611.5 42.0 %all-reduce.11.cloned.1.call-done = bf16[128,256]{1,0:T(8,128)(2,1)} async-done(((bf16[128,256]{1,0:T(8,128)(2,1)}), bf16[128,256]{1,0:T(8,128)(2,1)}) %all-reduce.11.cloned.1.call-update) | async-done | bytes 65552 | tf_op jit(solution)/shard_map/psum | solution.py:97
  (87 shorter events, 45.7 us)
Async XLA Ops:
  7.2 12.1 %copy-start = (bf16[128,256]{1,0:T(8,128)(2,1)S(1)}, bf16[128,256]{1,0:T(8,128)(2,1)}, u32[]{:S(2)}) copy-start(bf16[128,256]{1,0:T(8,128)(2,1)} %param.16) | copy-start | bytes 196612
  7.2 208.9 %reduce-scatter.15.cloned.1.call-start = ((), (), s32[]{:S(2)}) async-start(), calls=%async_computation.5 | async-start | bytes 557056 | tf_op jit(solution)/shard_map/reduce_scatter | solution.py:88
  20.8 285.4 %all-reduce.13.cloned.1.call-start = ((), (), s32[]{:S(2)}) async-start(), calls=%async_computation.7 | async-start | bytes 1376256 | tf_op jit(solution)/shard_map/psum | solution.py:97
  34.3 4.1 copy-start.3
  35.1 4.7 copy-start.4
  38.4 3.0 copy-start.12
  86.5 4.1 copy-start.13
  131.2 4.1 copy-start.14
  164.4 11.1 %copy-start.9 = (bf16[8,2048]{1,0:T(8,128)(2,1)S(1)}, bf16[8,2048]{1,0:T(8,128)(2,1)}, u32[]{:S(2)}) copy-start(bf16[8,2048]{1,0:T(8,128)(2,1)} %param.29) | copy-start | bytes 98308
  175.5 40.6 %copy-start.11 = (bf16[8,2048]{1,0:T(8,128)(2,1)S(1)}, bf16[8,2048]{1,0:T(8,128)(2,1)}, u32[]{:S(2)}) copy-start(bf16[8,2048]{1,0:T(8,128)(2,1)} %param.15) | copy-start | bytes 98308
  216.0 41.2 %copy-start.2 = (bf16[2048,896]{0,1:T(8,128)(2,1)S(1)}, bf16[2048,896]{0,1:T(8,128)(2,1)}, u32[]{:S(2)}) copy-start(bf16[2048,896]{0,1:T(8,128)(2,1)} %reshape.637) | copy-start | bytes 11010052
  259.2 174.7 %reduce-scatter.13.cloned.1.call-start = ((), (), s32[]{:S(2)}) async-start(), calls=%async_computation.3 | async-start | bytes 557056 | tf_op jit(solution)/shard_map/reduce_scatter | solution.py:88
  306.1 3.9 copy-start.5
  306.1 3.9 copy-start.6
  306.1 3.9 copy-start.7
  312.9 3.0 copy-start.1
  317.6 186.1 %reduce-scatter.17.cloned.1.call-start = ((), (), s32[]{:S(2)}) async-start(), calls=%async_computation.6 | async-start | bytes 557056 | tf_op jit(solution)/shard_map/reduce_scatter | solution.py:88
  391.8 212.6 %all-reduce.15.cloned.1.call-start = ((), (), s32[]{:S(2)}) async-start(), calls=%async_computation.8 | async-start | bytes 12582912
  431.3 0.7 copy-start.15
  431.4 222.2 %all-reduce.11.cloned.1.call-start = ((), (), s32[]{:S(2)}) async-start(), calls=%async_computation.4 | async-start | bytes 131072 | tf_op jit(solution)/shard_map/psum | solution.py:97
  434.7 40.6 %copy-start.10 = (bf16[8,2048]{1,0:T(8,128)(2,1)}, bf16[8,2048]{1,0:T(8,128)(2,1)S(1)}, u32[]{:S(2)}) copy-start(bf16[8,2048]{1,0:T(8,128)(2,1)S(1)} %add_convert_fusion) | copy-start | bytes 98308
  500.9 4.2 collective-permute-start
  604.4 3.1 copy-start.8
Sparse Core Ops, SparseCore 0:
  20.9 70.2 reduce-scatter.14
  259.3 46.7 all-reduce.12
  317.7 68.1 reduce-scatter.12
  391.9 68.2 reduce-scatter.16
  463.0 141.3 all-reduce.14
  607.1 46.3 all-reduce.10
where the time goes:
time: 675 us; the launch traced here: 662 us
  local copies, waits for them, and re-layouts  275 us (41%)
  waiting for transfers between devices  187 us (28%)
  blocking collectives  128 us (19%)
  matrix products  29.5 us (4%)
  other arithmetic  21.6 us (3%)
  between operations  18.9 us (3%)
    all_gather x3, blocking collectives, rows_over_out(): return lax.all_gather(local_rows, 'out', axis=0, tiled=True)  107 us
    unnamed x8, waiting for transfers between devices  98.3 us
    psum x2, waiting for transfers between devices, total_over_in(): lax.psum(as_sent(partials), 'in')  88.9 us
    reshape x8, local copies, waits for them, and re-layouts, pick_local(): shaped = matrix.reshape(block_rows, BLOCK, block_cols, BLOCK)  66.2 us
    gather x7, local copies, waits for them, and re-layouts, pick_local(): shaped[flat_ids // block_cols, :, flat_ids % block_cols, :]  41.5 us
    transpose x4, local copies, waits for them, and re-layouts, place_local(): filled.reshape(block_rows, block_cols, BLOCK, BLOCK).transpose(0, 2, 1, 3)  37.3 us
    reshape x4, local copies, waits for them, and re-layouts, place_local(): return filled.reshape(block_rows * BLOCK, block_cols * BLOCK)  36.6 us
    reshape x4, local copies, waits for them, and re-layouts, place_local(): filled.reshape(block_rows, block_cols, BLOCK, BLOCK).transpose(0, 2, 1, 3)  35.5 us
  transfers between devices with their start and end apart: 7, of which 3 were waited for; matrix products, arithmetic and copies ran while one was open for 47% of the time, Pallas kernels for 0%

commit v1 on v0

v1 whole, which is shorter than its diff:
```python
import jax
import jax.numpy as jnp
from jax import lax
from jax.experimental import pallas as pl
from jax.experimental.pallas import tpu as pltpu
from jax.sharding import PartitionSpec as P

BLOCK = 64
CELL = BLOCK * BLOCK
BF = jnp.bfloat16
F32 = jnp.float32
MESH = pl.DeviceIdType.MESH
VM = pl.BlockSpec(memory_space=pltpu.VMEM)
ANY = pl.BlockSpec(memory_space=pl.ANY)


def dot(a, b):
    return lax.dot_general(a, b, (((1,), (0,)), ((), ())), preferred_element_type=F32)


def dot_nt(a, b):
    return lax.dot_general(a, b, (((1,), (1,)), ((), ())), preferred_element_type=F32)


def dot_tn(a, b):
    return lax.dot_general(a, b, (((0,), (0,)), ((), ())), preferred_element_type=F32)


def one_hot(row, positions):
    spots = lax.broadcasted_iota(jnp.int32, (positions, row.shape[1]), 0)
    return jnp.where(spots == row, 1.0, 0.0).astype(BF)


def swap_matrix(inner, outer):
    rows = lax.broadcasted_iota(jnp.int32, (inner * outer, inner * outer), 0)
    cols = lax.broadcasted_iota(jnp.int32, (inner * outer, inner * outer), 1)
    source = (rows % outer) * inner + rows // outer
    return jnp.where(cols == source, 1.0, 0.0).astype(BF)


def halves(first, second):
    low = lax.broadcasted_iota(jnp.int32, first.shape, 1) < BLOCK
    return (
        jnp.where(low, first, pltpu.roll(second, BLOCK, 1)),
        jnp.where(low, pltpu.roll(first, BLOCK, 1), second),
    )


def place(hot, swap, blocks, stage, out, inner, used, row0):
    chunk = 256 // inner
    width = out.shape[1]

    def step(k, _):
        lanes = pl.ds(pl.multiple_of(k * chunk * BLOCK, chunk * BLOCK), chunk * BLOCK)
        flat = dot(hot, blocks[:, lanes])
        for p in range(chunk // 2):
            for q in range(width // 128):
                left = flat[2 * q * inner:(2 * q + 1) * inner, p * 128:(p + 1) * 128]
                right = flat[(2 * q + 1) * inner:(2 * q + 2) * inner, p * 128:(p + 1) * 128]
                pair = jnp.concatenate(halves(left, right), axis=0).astype(BF)
                stage[2 * p * inner:(2 * p + 2) * inner, q * 128:(q + 1) * 128] = pair
        dense = dot(swap, stage[:, :width]).astype(BF)
        for r in range(used):
            at = pl.multiple_of(row0 + r * BLOCK + k * chunk, 16)
            out[pl.ds(at, chunk), :] = dense[r * chunk:(r + 1) * chunk]
        return 0

    lax.fori_loop(0, BLOCK // chunk, step, 0)


def place_kernel(idx, gate, up, down, heads, context, wg, wu, wd, wh, term, stage):
    swap8 = swap_matrix(8, 32)
    swap16 = swap_matrix(16, 16)
    place(one_hot(idx[3:4, :heads.shape[0]], 256), swap8, heads, stage, wh, 8, 4, 0)
    for t in range(4):
        cols = slice(t * 512, (t + 1) * 512)
        term[:, cols] = dot(context[...], wh[:, cols]).astype(BF)
    slots = gate.shape[0]
    for row, blocks, out in ((0, gate, wg), (1, up, wu)):
        hot = one_hot(idx[row:row + 1, :slots], 448)
        for s in range(2):
            place(hot[s * 224:(s + 1) * 224], swap16, blocks, stage, out, 16, 16, s * 1024)
    place(one_hot(idx[2:3, :slots], 512), swap16, down, stage, wd, 16, 14, 0)


def place_call(idx, gate, up, down, heads, context):
    shapes = [
        jax.ShapeDtypeStruct((2048, 896), BF),
        jax.ShapeDtypeStruct((2048, 896), BF),
        jax.ShapeDtypeStruct((896, 2048), BF),
        jax.ShapeDtypeStruct((256, 2048), BF),
        jax.ShapeDtypeStruct((128, 2048), BF),
    ]
    return pl.pallas_call(
        place_kernel,
        out_shape=shapes,
        in_specs=[VM] * 6,
        out_specs=[VM] * 5,
        scratch_shapes=[pltpu.VMEM((256, 2048), BF)],
        compiler_params=pltpu.CompilerParams(vmem_limit_bytes=56 * 2**20),
        name="place",
    )(idx, gate, up, down, heads, context)


def pick(left, rights, hots, outs, flats, swap, turned, inner, used, stripes):
    chunk = 256 // inner
    span = used * BLOCK
    for s in range(stripes * span // 128):
        turned[s * 128:(s + 1) * 128, :] = left[:, s * 128:(s + 1) * 128].T

    def step(k, _):
        lanes = pl.ds(pl.multiple_of(k * chunk * BLOCK, chunk * BLOCK), chunk * BLOCK)
        for s in range(stripes):
            rows = [
                turned[pl.ds(pl.multiple_of(s * span + r * BLOCK + k * chunk, 16), chunk), :]
                for r in range(used)
            ]
            rows += [jnp.zeros_like(rows[0])] * (inner - used)
            ordered = dot(swap, jnp.concatenate(rows, axis=0)).astype(BF)
            for right, flat in zip(rights, flats):
                width = right.shape[1]
                base = s * (width // BLOCK) * inner
                piece = 512 if width % 512 == 0 else 896
                for t in range(width // piece):
                    grad = dot(ordered, right[:, t * piece:(t + 1) * piece])
                    for q in range(piece // 128):
                        for p in range(chunk // 2):
                            pair = grad[2 * p * inner:(2 * p + 2) * inner, q * 128:(q + 1) * 128]
                            both = jnp.concatenate(halves(pair[:inner], pair[inner:]), axis=0)
                            at = base + (t * piece // 128 + q) * 2 * inner
                            flat[at:at + 2 * inner, p * 128:(p + 1) * 128] = both.astype(BF)
        for hot, flat, out in zip(hots, flats, outs):
            depth = hot.shape[0]
            picked = dot_tn(hot, flat[:depth, :chunk * BLOCK])
            out[:, lanes] = picked[:out.shape[0]].astype(BF)
        return 0

    lax.fori_loop(0, BLOCK // chunk, step, 0)


def grads_kernel(idx, res, cot, ig, hid, gd, ud, ctx, og, ou, od, oh, turned, flat_a, flat_b):
    swap16 = swap_matrix(16, 16)

    def hot(row, positions):
        return one_hot(idx[row:row + 1, :128], positions)

    pick(res, (gd, ud), (hot(4, 448), hot(5, 448)), (og, ou), (flat_a, flat_b), swap16, turned, 16, 16, 2)
    pick(hid, (cot,), (hot(6, 512),), (od,), (flat_a,), swap16, turned, 16, 14, 1)
    pick(ctx, (ig,), (hot(7, 256),), (oh,), (flat_a,), swap_matrix(32, 8), turned, 8, 4, 1)


def grads_call(idx, res, cot, ig, hid, gd, ud, ctx):
    shapes = [jax.ShapeDtypeStruct((n, CELL), BF) for n in (60, 60, 60, 17)]
    return pl.pallas_call(
        grads_kernel,
        out_shape=shapes,
        in_specs=[VM] * 8,
        out_specs=[VM] * 4,
        scratch_shapes=[
            pltpu.VMEM((2048, 512), BF),
            pltpu.VMEM((512, 2048), BF),
            pltpu.VMEM((512, 2048), BF),
        ],
        compiler_params=pltpu.CompilerParams(vmem_limit_bytes=56 * 2**20),
        name="grads",
    )(idx, res, cot, ig, hid, gd, ud, ctx)


class Links:

    def __init__(self):
        self.dp, self.y, self.out = lax.axis_index("dp"), lax.axis_index("in"), lax.axis_index("out")
        self.depth = lax.axis_size("out") // 2
        self.tall = lax.axis_size("in")
        self.core, self.z = self.dp % 2, self.out // 2
        self.low = self.out % 2
        self.x = (self.dp // 2) * 2 + self.low

    def at_x(self, k):
        x = (self.x + k) % 4
        return (x // 2) * 2 + self.core, self.y, self.z * 2 + x % 2

    def at_z(self, k):
        return self.dp, self.y, ((self.z + k) % self.depth) * 2 + self.low

    def at_y(self, k):
        return self.dp, (self.y + k) % self.tall, self.out

    def sibling(self):
        return (self.dp // 2) * 2 + 1 - self.core, self.y, self.out

    def beside(self):
        return self.dp, self.y, self.z * 2 + 1 - self.low

    def across(self):
        return (self.dp + 2) % 4, self.y, self.out

    def greet(self):
        barrier = pltpu.get_barrier_semaphore()
        peers = [self.at_x(k) for k in (1, 2, 3)]
        peers += [self.at_z(k) for k in range(1, self.depth)]
        peers += [self.at_y(k) for k in range(1, self.tall)]
        peers += [self.sibling()]
        for peer in peers:
            pl.semaphore_signal(barrier, inc=1, device_id=peer, device_id_type=MESH)
        pl.semaphore_wait(barrier, len(peers))


def send(source, target, sems, k, to):
    copy = pltpu.make_async_remote_copy(
        src_ref=source,
        dst_ref=target,
        send_sem=sems.at[0, k],
        recv_sem=sems.at[1, k],
        device_id=to,
        device_id_type=MESH,
    )
    copy.start()
    return copy


class Spread:

    def __init__(self, me, whole, sems):
        self.me, self.whole, self.sems = me, whole, sems
        self.low = pl.ds(pl.multiple_of(me.low * 1024, 1024), 1024)

    def rows(self, dp):
        return pl.ds(pl.multiple_of(dp * 128, 128), 128)

    def over_z(self, own):
        me = self.me
        spot = self.whole.at[pl.ds(pl.multiple_of(me.dp * 128 + me.z * 16, 16), 16), self.low]
        spot[...] = own
        self.first = [send(spot, spot, self.sems, k - 1, me.at_z(k)) for k in range(1, me.depth)]

    def over_x(self):
        me = self.me
        for copy in self.first:
            copy.wait_recv()
        strip = self.whole.at[self.rows(me.dp), self.low]
        near = jnp.where(me.low == 0, 1, 3)
        self.near = send(strip, strip, self.sems, 7, me.beside())
        self.wide = [
            send(strip, strip, self.sems, 8, me.at_x(4 - near)),
            send(strip, strip, self.sems, 9, me.at_x(2)),
        ]

    def group(self):
        self.near.wait_recv()
        return self.rows(self.me.dp)

    def over_cores(self):
        me = self.me
        for copy in self.wide:
            copy.wait_recv()
        self.cores = []
        for k, dp in enumerate((me.dp, (me.dp + 2) % 4)):
            part = self.whole.at[self.rows(dp), :]
            self.cores.append(send(part, part, self.sems, 10 + k, me.sibling()))

    def finish(self):
        for copy in self.cores:
            copy.wait_recv()
        for copy in self.first + [self.near] + self.wide + self.cores:
            copy.wait_send()


class Collect:

    def __init__(self, me, term, half, sums, parts, sems):
        self.me, self.term, self.half, self.sums, self.parts, self.sems = me, term, half, sums, parts, sems

    def over_x(self):
        away = pl.ds(pl.multiple_of((1 - self.me.low) * 1024, 1024), 1024)
        self.near = send(self.term.at[:, away], self.half, self.sems, 7, self.me.beside())

    def over_z(self):
        me = self.me
        self.near.wait_recv()
        home = pl.ds(pl.multiple_of(me.low * 1024, 1024), 1024)
        self.sums[...] = (self.term[:, home].astype(F32) + self.half[...].astype(F32)).astype(BF)
        self.far = []
        for k in range(1, me.depth):
            z = (me.z + k) % me.depth
            chunk = self.sums.at[pl.ds(pl.multiple_of(z * 16, 16), 16), :]
            self.far.append(send(chunk, self.parts.at[k - 1], self.sems, k - 1, me.at_z(k)))

    def total(self):
        me = self.me
        rows = pl.ds(pl.multiple_of(me.z * 16, 16), 16)
        total = self.sums[rows, :].astype(F32)
        for k in range(1, me.depth):
            self.far[k - 1].wait_recv()
            total = total + self.parts[k - 1].astype(F32)
        return total

    def finish(self):
        self.near.wait_send()
        for copy in self.far:
            copy.wait_send()


def swap_out(me, total, outgoing, landing, sems, k):
    outgoing[...] = total
    away = outgoing.at[pl.ds(pl.multiple_of((1 - me.low) * 8, 8), 8), :]
    lanes = pl.ds(pl.multiple_of(me.low * 1024, 1024), 1024)
    landing[:, lanes] = outgoing[pl.ds(pl.multiple_of(me.low * 8, 8), 8), :]
    return send(away, landing.at[:, lanes], sems, k, me.beside())


def chain_kernel(
    x8, cot8, context, term, wg, wu, wd, wh,
    layer, input_grad, context_grad, res, cot, ig, mid, ctx,
    cells, edge, halves_in, sums, parts, backs,
    shares, shares_bf, gathered, swap_from, swap_to, near_sums,
    sem_res, sem_cot, sem_ig, sem_rs, sem_ctx, sem_sum, sem_mid, sem_cg, sem_swap,
):
    me = Links()
    me.greet()
    low8 = pl.ds(pl.multiple_of(me.low * 8, 8), 8)
    away = pl.ds(pl.multiple_of((1 - me.low) * 1024, 1024), 1024)
    home = pl.ds(pl.multiple_of(me.low * 1024, 1024), 1024)

    cells[0] = x8[...].astype(F32)
    cells[1] = cot8[...].astype(F32)
    edge[:, low8, :] = cells[:, :, home]
    entry = send(cells.at[:, :, away], edge.at[:, low8, :], sem_swap, 0, me.beside())
    attention = Collect(me, term, halves_in.at[0], sums.at[0], parts.at[0], sem_rs.at[0])
    attention.over_x()

    own_ctx = pl.ds(pl.multiple_of(me.dp * 128, 128), 128)
    ctx[own_ctx, :] = context[...]
    spot = ctx.at[own_ctx, :]
    ctx_copies = [send(spot, spot, sem_ctx, k, to) for k, to in enumerate((me.sibling(), me.across()))]

    entry.wait_recv()
    spread_cot = Spread(me, cot, sem_cot)
    spread_cot.over_z(edge[1].astype(BF))
    attention.over_z()
    spread_cot.over_x()

    residual = edge[0] + attention.total()
    spread_res = Spread(me, res, sem_res)
    spread_res.over_z(residual.astype(BF))

    def share(slot):
        copies = []
        for k in range(1, me.tall):
            rows = pl.ds(pl.multiple_of(((me.y + k) % me.tall) * 32, 32), 32)
            copies.append(
                send(shares_bf.at[slot, rows, :], gathered.at[k - 1, slot], sem_sum.at[slot], k - 1, me.at_y(k))
            )
        return copies

    rows = spread_cot.group()

    def grad_hidden(t, _):
        lanes = pl.ds(pl.multiple_of(t * 128, 128), 128)
        shares[2, :, lanes] = dot_nt(cot[rows, :], wd[lanes, :])
        return 0

    lax.fori_loop(0, 7, grad_hidden, 0)
    shares_bf[2] = shares[2].astype(BF)
    spread_res.over_x()
    sum_copies = {2: share(2)}

    rows = spread_res.group()
    for slot, weight in ((0, wg), (1, wu)):

        def fan(t, _, weight=weight, slot=slot):
            lanes = pl.ds(pl.multiple_of(t * 128, 128), 128)
            shares[slot, :, lanes] = dot(res[rows, :], weight[:, lanes])
            return 0

        lax.fori_loop(0, 7, fan, 0)
        shares_bf[slot] = shares[slot].astype(BF)
        sum_copies[slot] = share(slot)

    spread_cot.over_cores()
    quarter = pl.ds(pl.multiple_of(me.y * 32, 32), 32)
    totals = []
    for slot in (2, 0, 1):
        total = shares[slot, quarter, :]
        for k in range(me.tall - 1):
            sum_copies[slot][k].wait_recv()
            total = total + gathered[k, slot].astype(F32)
        totals.append(total)
    hidden_grad, gate_sum, up_sum = totals
    sigmoid = 1.0 / (1.0 + jnp.exp(-gate_sum))
    spot_rows = pl.ds(pl.multiple_of(me.dp * 128 + me.y * 32, 32), 32)
    mid[0, spot_rows, :] = (gate_sum * sigmoid * up_sum).astype(BF)
    mid[1, spot_rows, :] = (
        hidden_grad * up_sum * sigmoid * (1.0 + gate_sum * (1.0 - sigmoid))
    ).astype(BF)
    mid[2, spot_rows, :] = (hidden_grad * gate_sum * sigmoid).astype(BF)
    spot = mid.at[:, spot_rows, :]
    mid_copies = [send(spot, spot, sem_mid, k - 1, me.at_y(k)) for k in range(1, me.tall)]
    mid_across = send(spot, spot, sem_mid, 3, me.across())
    spread_res.over_cores()
    for copy in mid_copies:
        copy.wait_recv()

    rows = pl.ds(pl.multiple_of(me.dp * 128, 128), 128)

    def back(t, _):
        lanes = pl.ds(pl.multiple_of(t * 256, 256), 256)
        backs[0, :, lanes] = (
            dot_nt(mid[1, rows, :], wg[lanes, :]) + dot_nt(mid[2, rows, :], wu[lanes, :])
        ).astype(BF)
        return 0

    lax.fori_loop(0, 8, back, 0)
    backward = Collect(me, backs.at[0], halves_in.at[1], sums.at[1], parts.at[1], sem_rs.at[1])
    backward.over_x()

    def forth(t, _):
        lanes = pl.ds(pl.multiple_of(t * 256, 256), 256)
        backs[1, :, lanes] = dot(mid[0, rows, :], wd[:, lanes]).astype(BF)
        return 0

    lax.fori_loop(0, 8, forth, 0)
    forward = Collect(me, backs.at[1], halves_in.at[2], sums.at[2], parts.at[2], sem_rs.at[2])
    forward.over_x()
    backward.over_z()
    forward.over_z()

    mid_across.wait_recv()
    spot = mid.at[:, pl.ds(pl.multiple_of(((me.dp + 2) % 4) * 128 + me.y * 32, 32), 32), :]
    mid_far = [send(spot, spot, sem_mid, 3 + k, me.at_y(k)) for k in range(1, me.tall)]

    total = edge[1] + backward.total()
    spread_ig = Spread(me, ig, sem_ig)
    spread_ig.over_z(total.astype(BF))
    swap_ig = swap_out(me, total, swap_from.at[0], swap_to.at[0], sem_swap, 1)
    total = residual.astype(BF).astype(F32) + forward.total()
    swap_layer = swap_out(me, total, swap_from.at[1], swap_to.at[1], sem_swap, 2)

    for copy in mid_far:
        copy.wait_recv()
    mid_cores = []
    for k, dp in enumerate((me.dp, (me.dp + 2) % 4)):
        spot = mid.at[:, pl.ds(pl.multiple_of(dp * 128, 128), 128), :]
        mid_cores.append(send(spot, spot, sem_mid, 7 + k, me.sibling()))

    spread_ig.over_x()
    rows = spread_ig.group()
    near_sums[me.y] = dot_nt(ig[rows, :], wh[...]).astype(BF)
    spot = near_sums.at[me.y]
    cg_copies = [send(spot, spot, sem_cg, k - 1, me.at_y(k)) for k in range(1, me.tall)]

    ctx_copies[1].wait_recv()
    spot = ctx.at[pl.ds(pl.multiple_of(((me.dp + 2) % 4) * 128, 128), 128), :]
    ctx_copies.append(send(spot, spot, sem_ctx, 2, me.sibling()))
    swap_ig.wait_recv()
    input_grad[...] = swap_to[0].astype(BF)
    swap_layer.wait_recv()
    layer[...] = swap_to[1].astype(BF)
    spread_ig.over_cores()

    for copy in cg_copies:
        copy.wait_recv()
    total = near_sums[0].astype(F32)
    for k in range(1, me.tall):
        total = total + near_sums[k].astype(F32)
    context_grad[...] = total.astype(BF)

    for spread in (spread_cot, spread_res, spread_ig):
        spread.finish()
    for collect in (attention, backward, forward):
        collect.finish()
    for copy in mid_cores + [ctx_copies[0], ctx_copies[2]]:
        copy.wait_recv()
    late = [entry, swap_ig, swap_layer, mid_across]
    late += ctx_copies + mid_copies + mid_far + mid_cores + cg_copies
    for slot in range(3):
        late += sum_copies[slot]
    for copy in late:
        copy.wait_send()


def chain_call(x8, cot8, context, term, wg, wu, wd, wh):
    def sds(*shape):
        return jax.ShapeDtypeStruct(shape, BF)

    shapes = [
        sds(8, 2048), sds(8, 2048), sds(128, 256),
        sds(512, 2048), sds(512, 2048), sds(512, 2048), sds(3, 512, 896), sds(512, 256),
    ]
    dma = pltpu.SemaphoreType.DMA
    tall = lax.axis_size("in")
    depth = lax.axis_size("out") // 2
    return pl.pallas_call(
        chain_kernel,
        out_shape=shapes,
        in_specs=[VM] * 8,
        out_specs=[VM] * 8,
        scratch_shapes=[
            pltpu.VMEM((2, 8, 2048), F32),
            pltpu.VMEM((2, 16, 1024), F32),
            pltpu.VMEM((3, 128, 1024), BF),
            pltpu.VMEM((3, 128, 1024), BF),
            pltpu.VMEM((3, depth - 1, 16, 1024), BF),
            pltpu.VMEM((2, 128, 2048), BF),
            pltpu.VMEM((3, 128, 896), F32),
            pltpu.VMEM((3, 128, 896), BF),
            pltpu.VMEM((tall - 1, 3, 32, 896), BF),
            pltpu.VMEM((2, 16, 1024), F32),
            pltpu.VMEM((2, 8, 2048), F32),
            pltpu.VMEM((tall, 128, 256), BF),
            dma((2, 12)),
            dma((2, 12)),
            dma((2, 12)),
            dma((3, 2, 8)),
            dma((2, 3)),
            dma((3, 2, 3)),
            dma((2, 9)),
            dma((2, 3)),
            dma((2, 3)),
        ],
        compiler_params=pltpu.CompilerParams(
            collective_id=0, has_side_effects=True, vmem_limit_bytes=56 * 2**20
        ),
        name="chain",
    )(x8, cot8, context, term, wg, wu, wd, wh)


def positions(ids, count, share, dp, spots):
    count = count.reshape(())
    flat = jnp.where(jnp.arange(ids.shape[-1], dtype=jnp.int32) < count, spots(ids.reshape(-1)), -1)
    own = lax.dynamic_slice(flat, (dp * share,), (share,))
    pad = lambda row: jnp.pad(row, (0, 256 - row.shape[0]), constant_values=-1)
    return pad(flat), pad(own)


def local(
    inputs, context,
    gate_blocks, gate_ids, gate_count,
    up_blocks, up_ids, up_count,
    down_blocks, down_ids, down_count,
    heads_blocks, heads_ids, heads_count,
    cotangent,
):
    dp = lax.axis_index("dp")
    tall = lambda i: (i // 224) * 224 + (i % 14) * 16 + (i // 14) % 16
    pairs = [
        positions(gate_ids, gate_count, 60, dp, tall),
        positions(up_ids, up_count, 60, dp, tall),
        positions(down_ids, down_count, 60, dp, lambda i: (i % 32) * 16 + i // 32),
        positions(heads_ids, heads_count, 17, dp, lambda i: (i % 32) * 8 + i // 32),
    ]
    idx = jnp.stack([p[0] for p in pairs] + [p[1] for p in pairs])
    rows = lambda blocks: blocks.reshape(-1, CELL)
    wg, wu, wd, wh, term = place_call(
        idx, rows(gate_blocks), rows(up_blocks), rows(down_blocks), rows(heads_blocks), context
    )
    layer, input_grad, context_grad, res, cot, ig, mid, ctx = chain_call(
        inputs, cotangent, context, term, wg, wu, wd, wh
    )
    grads = grads_call(idx, res, cot, ig, mid[0], mid[1], mid[2], ctx)
    return (layer, input_grad, context_grad, *(g.reshape(1, 1, -1, CELL) for g in grads))


def solution(mesh):
    rows = P(("dp", "out"), "in")
    tall, wide = ("in", "out"), ("out", "in")

    def lists(axes):
        return P(*axes, None, None), P(*axes, None), P(*axes)

    return jax.shard_map(
        local,
        mesh=mesh,
        in_specs=(rows, P("dp", "out"), *lists(tall), *lists(tall), *lists(wide), *lists(wide), rows),
        out_specs=(
            rows,
            rows,
            P("dp", "out"),
            P(*tall, "dp", None),
            P(*tall, "dp", None),
            P(*wide, "dp", None),
            P(*wide, "dp", None),
        ),
        check_vma=False,
    )
```

time: 675 us -> 163 us (0.24); the launches traced: 662 us -> 160 us
  local copies, waits for them, and re-layouts: 275 us -> 6.16 us
  waiting for transfers between devices: 187 us -> 0 us
  Pallas kernels: 0 us -> 147 us
  blocking collectives: 128 us -> 0 us
  matrix products: 29.5 us -> 0 us
  other arithmetic: 21.6 us -> 4.19 us
  between operations: 18.9 us -> 3.27 us
    pallas_call x0 -> x3, Pallas kernels: none -> 147 us  [the longest x1 102 us: chain_call(): pl.pallas_call(chain_kernel, out_shape=shapes, in_specs=[VM] * 8, out_spe...]
    reshape x20 -> x0, local copies, waits for them, and re-layouts: 143 us -> none  [the longest x8 66.2 us: pick_local(): shaped = matrix.reshape(block_rows, BLOCK, block_cols, BLOCK)]
    all_gather x3 -> x0, blocking collectives: 107 us -> none  [rows_over_out(): return lax.all_gather(local_rows, 'out', axis=0, tiled=True)]
    unnamed x8 -> x0, waiting for transfers between devices: 98.3 us -> none
    psum x2 -> x0, waiting for transfers between devices: 88.9 us -> none  [total_over_in(): lax.psum(as_sent(partials), 'in')]
    gather x7 -> x0, local copies, waits for them, and re-layouts: 41.5 us -> none  [pick_local(): shaped[flat_ids // block_cols, :, flat_ids % block_cols, :]]
    transpose x4 -> x0, local copies, waits for them, and re-layouts: 37.3 us -> none  [place_local(): filled.reshape(block_rows, block_cols, BLOCK, BLOCK).transpose(0, 2, 1, 3)]
    dot_general x12 -> x0, matrix products: 29.5 us -> none  [the longest x4 9.64 us: product_nt(): lax.dot_general(left_side, right_side, (((1,), (1,)), ((), ())), preferre...]
  transfers between devices with their start and end apart: 7 -> 0, of which waited for: 3 -> 0; matrix products, arithmetic and copies ran while one was open for 47% -> 0% of each run, Pallas kernels for 0% -> 0%
where the time goes in v1:
time: 163 us; the launch traced here: 160 us
  Pallas kernels  147 us (90%)
  local copies, waits for them, and re-layouts  6.16 us (4%)
  other arithmetic  4.19 us (3%)
  between operations  3.27 us (2%)
    pallas_call x1, Pallas kernels, chain_call(): pl.pallas_call(chain_kernel, out_shape=shapes, in_specs=[VM] * 8, out_spe...  102 us
    pallas_call x1, Pallas kernels, place_call(): pl.pallas_call(place_kernel, out_shape=shapes, in_specs=[VM] * 6, out_spe...  24.6 us
    pallas_call x1, Pallas kernels, grads_call(): pl.pallas_call(grads_kernel, out_shape=shapes, in_specs=[VM] * 8, out_spe...  20.2 us
    squeeze x1, local copies, waits for them, and re-layouts, local(): grads = grads_call(idx, res, cot, ig, mid[0], mid[1], mid[2], ctx)  3.33 us

profile of v1, /device:TPU:2, one launch (start us, length us, event | category | flops | bytes accessed | tf_op | source)
XLA Modules:
  0.0 160.4 jit_solution(16970528750799776087)
XLA Ops:
  3.2 0.7 compare_select_fusion.4
  3.9 0.1 dynamic_slice.15
  4.0 0.7 compare_select_fusion.5
  4.7 0.1 dynamic_slice.14
  4.8 0.7 compare_reduce_fusion.2
  5.5 0.7 compare_reduce_fusion
  6.2 0.7 broadcast_divide_fusion.1
  6.9 0.1 dynamic_slice.12
  7.0 0.7 broadcast_divide_fusion
  7.7 0.1 dynamic_slice.13
  7.8 0.6 stack.35.idx
  8.4 24.6 %place.1 = (bf16[2048,896]{1,0:T(8,128)(2,1)}, bf16[2048,896]{1,0:T(8,128)(2,1)}, bf16[896,2048]{1,0:T(8,128)(2,1)}, bf16[256,2048]{1,0:T(8,128)(2,1)}, bf16[128,2048]{1,0:T(8,128)(2,1)}) custom-call(s32[8,256]{1,0:T(8,128)} %stack.35.idx, bf16[240,4096]{1,0:T(8,128)(2,1)} %bitcast.50, bf16[240,4096]{1,0:T(8,128)(2,1)} %bitcast.51, ...), custom_call_target="tpu_custom_call" | custom-call | tf_op jit(solution)/shard_map/place/pallas_call | solution.py:94
  33.0 101.9 %chain.1 = (bf16[8,2048]{1,0:T(8,128)(2,1)}, bf16[8,2048]{1,0:T(8,128)(2,1)}, bf16[128,256]{1,0:T(8,128)(2,1)}, bf16[512,2048]{1,0:T(8,128)(2,1)}, bf16[512,2048...) custom-call(bf16[8,2048]{1,0:T(8,128)(2,1)} %x8.1, ...), custom_call_target="tpu_custom_call" | custom-call | tf_op jit(solution)/shard_map/chain/pallas_call | solution.py:493
  135.0 3.3 %slice_bitcast_fusion = (bf16[512,896]{1,0:T(8,128)(2,1)}, bf16[512,896]{1,0:T(8,128)(2,1)}, bf16[512,896]{1,0:T(8,128)(2,1)}) fusion(bf16[3,512,896]{2,1,0:T(8,128)(2,1)} %get-tuple-element.35), kind=kLoop, calls=%fused_computation | loop fusion | bytes 5505024 | tf_op jit(solution)/shard_map/squeeze | solution.py:560
  138.3 0.0 copy-start.2
  138.3 0.0 copy-start.1
  138.3 0.0 copy-start
  138.3 20.2 %grads.1 = (bf16[60,4096]{1,0:T(8,128)(2,1)}, bf16[60,4096]{1,0:T(8,128)(2,1)}, bf16[60,4096]{1,0:T(8,128)(2,1)}, bf16[17,4096]{1,0:T(8,128)(2,1)}) custom-call(s32[8,256]{1,0:T(8,128)} %stack.35.idx, bf16[512,2048]{1,0:T(8,128)(2,1)} %get-tuple-element.32.res, bf16[512,2048]{1,0:T(8,128)(2,1)} %get-tuple-element.33.cot, ...), custom_call_target="tpu_custom_call" | custom-call | tf_op jit(solution)/shard_map/grads/pallas_call | solution.py:154
  158.5 0.0 copy-done.2
  158.5 0.6 copy.29
  159.2 0.0 copy-done.1
  159.2 0.6 copy.30
  159.8 0.0 copy-done
  159.8 0.6 copy.31
  (10 shorter events, 0.1 us)
Async XLA Ops:
  138.3 20.2 %copy-start.2 = (bf16[8,2048]{1,0:T(8,128)(2,1)S(1)}, bf16[8,2048]{1,0:T(8,128)(2,1)}, u32[]{:S(2)}) copy-start(bf16[8,2048]{1,0:T(8,128)(2,1)} %get-tuple-element.61) | copy-start | bytes 98308
  138.3 20.9 %copy-start.1 = (bf16[8,2048]{1,0:T(8,128)(2,1)S(1)}, bf16[8,2048]{1,0:T(8,128)(2,1)}, u32[]{:S(2)}) copy-start(bf16[8,2048]{1,0:T(8,128)(2,1)} %get-tuple-element.62) | copy-start | bytes 98308
  138.3 21.5 %copy-start = (bf16[128,256]{1,0:T(8,128)(2,1)S(1)}, bf16[128,256]{1,0:T(8,128)(2,1)}, u32[]{:S(2)}) copy-start(bf16[128,256]{1,0:T(8,128)(2,1)} %get-tuple-element.63) | copy-start | bytes 196612

commit v2 on v1

v2 whole, which is shorter than its diff:
```python
import jax
import jax.numpy as jnp
from jax import lax
from jax.experimental import pallas as pl
from jax.experimental.pallas import tpu as pltpu
from jax.sharding import PartitionSpec as P

BLOCK = 64
CELL = BLOCK * BLOCK
BF = jnp.bfloat16
F32 = jnp.float32
MESH = pl.DeviceIdType.MESH
VM = pl.BlockSpec(memory_space=pltpu.VMEM)
ANY = pl.BlockSpec(memory_space=pl.ANY)


def dot(a, b):
    return lax.dot_general(a, b, (((1,), (0,)), ((), ())), preferred_element_type=F32)


def dot_nt(a, b):
    return lax.dot_general(a, b, (((1,), (1,)), ((), ())), preferred_element_type=F32)


def dot_tn(a, b):
    return lax.dot_general(a, b, (((0,), (0,)), ((), ())), preferred_element_type=F32)


def one_hot(row, positions):
    spots = lax.broadcasted_iota(jnp.int32, (positions, row.shape[1]), 0)
    return jnp.where(spots == row, 1.0, 0.0).astype(BF)


def swap_matrix(inner, outer):
    rows = lax.broadcasted_iota(jnp.int32, (inner * outer, inner * outer), 0)
    cols = lax.broadcasted_iota(jnp.int32, (inner * outer, inner * outer), 1)
    source = (rows % outer) * inner + rows // outer
    return jnp.where(cols == source, 1.0, 0.0).astype(BF)


def halves(first, second):
    low = lax.broadcasted_iota(jnp.int32, first.shape, 1) < BLOCK
    return (
        jnp.where(low, first, pltpu.roll(second, BLOCK, 1)),
        jnp.where(low, pltpu.roll(first, BLOCK, 1), second),
    )


def spots(ids, count, kind):
    i = ids[...]
    if kind == "tall":
        r = (i * 2341) >> 15
        c = i - 14 * r
        spot = (r >> 4) * 224 + c * 16 + (r & 15)
    elif kind == "wide":
        spot = (i & 31) * 16 + (i >> 5)
    else:
        spot = (i & 31) * 8 + (i >> 5)
    slots = lax.broadcasted_iota(jnp.int32, i.shape, 1)
    return jnp.where(slots < count[...], spot, -1)


def place(hot, swap, blocks, stage, out, inner, used, stripes, k):
    chunk = 256 // inner
    width = out.shape[1]
    per = (width // BLOCK) * inner
    flat = dot(hot, blocks[:, k * chunk * BLOCK:(k + 1) * chunk * BLOCK]).astype(BF)
    for s in range(stripes):
        for p in range(chunk // 2):
            for q in range(width // 128):
                at = s * per + 2 * q * inner
                left = flat[at:at + inner, p * 128:(p + 1) * 128]
                right = flat[at + inner:at + 2 * inner, p * 128:(p + 1) * 128]
                pair = jnp.concatenate(halves(left, right), axis=0)
                at = s * 256 + 2 * p * inner
                stage[at:at + 2 * inner, q * 128:(q + 1) * 128] = pair
        dense = dot(swap, stage[s * 256:(s + 1) * 256, :width]).astype(BF)
        for r in range(used):
            at = s * inner * BLOCK + r * BLOCK + k * chunk
            out[at:at + chunk, :] = dense[r * chunk:(r + 1) * chunk]


def pick(left, rights, hots, outs, flats, swap, turned, inner, used, stripes):
    chunk = 256 // inner
    span = used * BLOCK
    for s in range(stripes * span // 128):
        turned[s * 128:(s + 1) * 128, :] = left[:, s * 128:(s + 1) * 128].T

    def step(k, _):
        lanes = pl.ds(pl.multiple_of(k * chunk * BLOCK, chunk * BLOCK), chunk * BLOCK)
        for s in range(stripes):
            rows = [
                turned[pl.ds(pl.multiple_of(s * span + r * BLOCK + k * chunk, 16), chunk), :]
                for r in range(used)
            ]
            rows += [jnp.zeros_like(rows[0])] * (inner - used)
            ordered = dot(swap, jnp.concatenate(rows, axis=0)).astype(BF)
            for right, flat in zip(rights, flats):
                width = right.shape[1]
                base = s * (width // BLOCK) * inner
                piece = 512 if width % 512 == 0 else 896
                for t in range(width // piece):
                    grad = dot(ordered, right[:, t * piece:(t + 1) * piece])
                    for q in range(piece // 128):
                        for p in range(chunk // 2):
                            pair = grad[2 * p * inner:(2 * p + 2) * inner, q * 128:(q + 1) * 128]
                            both = jnp.concatenate(halves(pair[:inner], pair[inner:]), axis=0)
                            at = base + (t * piece // 128 + q) * 2 * inner
                            flat[at:at + 2 * inner, p * 128:(p + 1) * 128] = both.astype(BF)
        for hot, flat, out in zip(hots, flats, outs):
            depth = hot.shape[0]
            picked = dot_tn(hot, flat[:depth, :chunk * BLOCK])
            out[:, lanes] = picked.astype(BF)
        return 0

    lax.fori_loop(0, BLOCK // chunk, step, 0)


def grads_kernel(
    gids, gcount, uids, ucount, dids, dcount, hids, hcount, res, cot, ig, mid, ctx,
    og, ou, od, oh, turned, flat_a, flat_b,
):
    swap16 = swap_matrix(16, 16)
    dp = lax.axis_index("dp")

    def hot(ids, count, kind, positions, share):
        spot = spots(ids, count, kind)
        own = spot[:, :share]
        for k in range(1, 4):
            own = jnp.where(dp == k, spot[:, k * share:(k + 1) * share], own)
        return one_hot(own, positions)

    hots = (hot(gids, gcount, "tall", 448, 60), hot(uids, ucount, "tall", 448, 60))
    pick(res, (mid.at[1], mid.at[2]), hots, (og, ou), (flat_a, flat_b), swap16, turned, 16, 16, 2)
    hots = (hot(dids, dcount, "wide", 512, 60),)
    pick(mid.at[0], (cot,), hots, (od,), (flat_a,), swap16, turned, 16, 14, 1)
    hots = (hot(hids, hcount, "heads", 256, 17),)
    pick(ctx, (ig,), hots, (oh,), (flat_a,), swap_matrix(32, 8), turned, 8, 4, 1)


def grads_call(lists, res, cot, ig, mid, ctx):
    shapes = [jax.ShapeDtypeStruct((n, CELL), BF) for n in (60, 60, 60, 17)]
    return pl.pallas_call(
        grads_kernel,
        out_shape=shapes,
        in_specs=[VM] * 13,
        out_specs=[VM] * 4,
        scratch_shapes=[
            pltpu.VMEM((2048, 512), BF),
            pltpu.VMEM((512, 2048), BF),
            pltpu.VMEM((512, 2048), BF),
        ],
        compiler_params=pltpu.CompilerParams(vmem_limit_bytes=56 * 2**20),
        name="grads",
    )(*lists, res, cot, ig, mid, ctx)


class Links:

    def __init__(self):
        self.dp, self.y, self.out = lax.axis_index("dp"), lax.axis_index("in"), lax.axis_index("out")
        self.depth = lax.axis_size("out") // 2
        self.tall = lax.axis_size("in")
        self.core, self.z = self.dp % 2, self.out // 2
        self.low = self.out % 2
        self.x = (self.dp // 2) * 2 + self.low

    def at_x(self, k):
        x = (self.x + k) % 4
        return (x // 2) * 2 + self.core, self.y, self.z * 2 + x % 2

    def at_z(self, k):
        return self.dp, self.y, ((self.z + k) % self.depth) * 2 + self.low

    def at_y(self, k):
        return self.dp, (self.y + k) % self.tall, self.out

    def sibling(self):
        return (self.dp // 2) * 2 + 1 - self.core, self.y, self.out

    def beside(self):
        return self.dp, self.y, self.z * 2 + 1 - self.low

    def across(self):
        return (self.dp + 2) % 4, self.y, self.out

    def greet(self):
        barrier = pltpu.get_barrier_semaphore()
        peers = [self.at_x(k) for k in (1, 2, 3)]
        peers += [self.at_z(k) for k in range(1, self.depth)]
        peers += [self.at_y(k) for k in range(1, self.tall)]
        peers += [self.sibling()]
        for peer in peers:
            pl.semaphore_signal(barrier, inc=1, device_id=peer, device_id_type=MESH)
        return barrier, len(peers)

    def meet(self, greeted):
        pl.semaphore_wait(*greeted)


def send(source, target, sems, k, to):
    copy = pltpu.make_async_remote_copy(
        src_ref=source,
        dst_ref=target,
        send_sem=sems.at[0, k],
        recv_sem=sems.at[1, k],
        device_id=to,
        device_id_type=MESH,
    )
    copy.start()
    return copy


class Spread:

    def __init__(self, me, whole, sems):
        self.me, self.whole, self.sems = me, whole, sems
        self.home = pl.ds(pl.multiple_of(me.low * 1024, 1024), 1024)
        self.away = pl.ds(pl.multiple_of((1 - me.low) * 1024, 1024), 1024)
        self.other = (me.dp + 2) % 4
        self.far = me.at_x(jnp.where(me.low == 0, 3, 1))
        self.sent = []

    def rows(self, dp, start=0, size=128):
        return pl.ds(pl.multiple_of(dp * 128 + start, 16), size)

    def move(self, rows, lanes, k, to):
        spot = self.whole.at[rows, lanes]
        copy = send(spot, spot, self.sems, k, to)
        self.sent.append(copy)
        return copy

    def chunk(self, z):
        return pl.ds(pl.multiple_of(self.me.dp * 128 + (z % self.me.depth) * 16, 16), 16)

    def over_z(self, own):
        me = self.me
        self.whole[self.chunk(me.z), self.home] = own
        self.first = {k: self.move(self.chunk(me.z), self.home, k, me.at_z(k)) for k in range(1, me.depth)}

    def over_x(self):
        me, depth = self.me, self.me.depth
        self.near = [self.move(self.chunk(me.z), self.home, 8, me.beside())]
        for k in sorted(range(1, depth), key=lambda k: min(k, depth - k)):
            self.first[k].wait_recv()
            self.near.append(self.move(self.chunk(me.z + depth - k), self.home, 8 + k, me.beside()))
        self.wide = self.move(self.rows(me.dp), self.home, 16, self.far)

    def group(self):
        for copy in self.near:
            copy.wait_recv()
        return self.rows(self.me.dp)

    def forward(self):
        me = self.me
        self.half_a = self.move(self.rows(me.dp, 0, 64), self.away, 17, self.far)
        self.cores = [self.move(self.rows(me.dp), slice(None), 19, me.sibling())]
        self.wide.wait_recv()
        self.half_b = self.move(self.rows(self.other, 64, 64), self.away, 18, me.beside())

    def over_cores(self):
        self.half_a.wait_recv()
        self.half_b.wait_recv()
        self.cores.append(self.move(self.rows(self.other), slice(None), 20, self.me.sibling()))

    def finish(self):
        for copy in self.cores:
            copy.wait_recv()

    def drain(self):
        for copy in self.sent:
            copy.wait_send()


class Collect:

    def __init__(self, me, term, half, sums, parts, sems):
        self.me, self.term, self.half, self.sums, self.parts, self.sems = me, term, half, sums, parts, sems
        self.order = sorted(range(me.depth), key=lambda k: -min(k, me.depth - k))

    def chunk(self, k):
        return pl.ds(pl.multiple_of(((self.me.z + k) % self.me.depth) * 16, 16), 16)

    def over_x(self):
        away = pl.ds(pl.multiple_of((1 - self.me.low) * 1024, 1024), 1024)
        self.near = {}
        for k in self.order:
            rows = self.chunk(k)
            self.near[k] = send(self.term.at[rows, away], self.half.at[rows, :], self.sems, 8 + k, self.me.beside())

    def over_z(self):
        me = self.me
        home = pl.ds(pl.multiple_of(me.low * 1024, 1024), 1024)
        self.far = {}
        for k in self.order:
            rows = self.chunk(k)
            self.near[k].wait_recv()
            both = self.term[rows, home].astype(F32) + self.half[rows, :].astype(F32)
            if k == 0:
                self.own = both
            else:
                self.sums[rows, :] = both.astype(BF)
                self.far[k] = send(self.sums.at[rows, :], self.parts.at[k - 1], self.sems, k, me.at_z(k))

    def total(self):
        total = self.own
        for k in reversed(self.order[:-1]):
            self.far[k].wait_recv()
            total = total + self.parts[k - 1].astype(F32)
        return total

    def drain(self):
        for copy in list(self.near.values()) + list(self.far.values()):
            copy.wait_send()


def swap_out(me, total, outgoing, landing, sems, k):
    outgoing[...] = total
    away = outgoing.at[pl.ds(pl.multiple_of((1 - me.low) * 8, 8), 8), :]
    lanes = pl.ds(pl.multiple_of(me.low * 1024, 1024), 1024)
    landing[:, lanes] = outgoing[pl.ds(pl.multiple_of(me.low * 8, 8), 8), :]
    return send(away, landing.at[:, lanes], sems, k, me.beside())


def chain_kernel(
    x8, cot8, context, gids, gcount, uids, ucount, dids, dcount, hids, hcount, gate, up, down, heads,
    layer, input_grad, context_grad, res, cot, ig, mid, ctx,
    gate_in, up_in, down_in, stage, wg, wu, wd, wh, term,
    cells, edge, halves_in, sums, parts, backs,
    shares, shares_bf, gathered, swap_from, swap_to, near_sums,
    sem_in, sem_res, sem_cot, sem_ig, sem_rs, sem_ctx, sem_sum, sem_mid, sem_cg, sem_swap,
):
    loads = []
    for k, (source, target) in enumerate(((gate, gate_in), (up, up_in), (down, down_in))):
        loads.append(pltpu.make_async_copy(source, target, sem_in.at[k]))
        loads[-1].start()
    me = Links()
    greeted = me.greet()
    hot = one_hot(spots(hids, hcount, "heads"), 256)
    swap = swap_matrix(8, 32)
    for k in range(2):
        place(hot, swap, heads, stage, wh, 8, 4, 1, k)
    for t in range(2):
        cols = slice(t * 1024, (t + 1) * 1024)
        term[:, cols] = dot(context[...], wh[:, cols]).astype(BF)

    swap16 = swap_matrix(16, 16)
    work = []

    def queue(load, ids, count, kind, blocks, out, stripes, used):
        held = {}

        def step(k):
            if k == 0:
                loads[load].wait()
                held["hot"] = one_hot(spots(ids, count, kind), 448 if kind == "tall" else 512)
            place(held["hot"], swap16, blocks, stage, out, 16, used, stripes, k)

        for k in range(4):
            work.append(lambda k=k: step(k))

    queue(0, gids, gcount, "tall", gate_in, wg, 2, 16)
    queue(1, uids, ucount, "tall", up_in, wu, 2, 16)
    queue(2, dids, dcount, "wide", down_in, wd, 1, 14)

    def fill(n):
        for _ in range(n):
            work.pop(0)()

    low8 = pl.ds(pl.multiple_of(me.low * 8, 8), 8)
    away = pl.ds(pl.multiple_of((1 - me.low) * 1024, 1024), 1024)
    home = pl.ds(pl.multiple_of(me.low * 1024, 1024), 1024)

    def collect(term, k):
        return Collect(me, term, halves_in.at[k], sums.at[k], parts.at[k], sem_rs.at[k])

    cells[0] = x8[...].astype(F32)
    cells[1] = cot8[...].astype(F32)
    edge[:, low8, :] = cells[:, :, home]
    me.meet(greeted)
    attention = collect(term, 0)
    attention.over_x()
    entry = send(cells.at[:, :, away], edge.at[:, low8, :], sem_swap, 0, me.beside())
    fill(3)
    attention.over_z()
    entry.wait_recv()
    spread_cot = Spread(me, cot, sem_cot)
    spread_cot.over_z(edge[1].astype(BF))
    own_ctx = pl.ds(pl.multiple_of(me.dp * 128, 128), 128)
    ctx[own_ctx, :] = context[...]
    spot = ctx.at[own_ctx, :]
    ctx_copies = [send(spot, spot, sem_ctx, k, to) for k, to in enumerate((me.sibling(), me.across()))]
    fill(3)
    residual = edge[0] + attention.total()
    spread_res = Spread(me, res, sem_res)
    spread_res.over_z(residual.astype(BF))
    spread_cot.over_x()
    fill(2)
    spread_res.over_x()
    fill(4)

    def share(slot):
        copies = []
        for k in range(1, me.tall):
            rows = pl.ds(pl.multiple_of(((me.y + k) % me.tall) * 32, 32), 32)
            copies.append(
                send(shares_bf.at[slot, rows, :], gathered.at[k - 1, slot], sem_sum.at[slot], k - 1, me.at_y(k))
            )
        return copies

    rows = spread_cot.group()
    for t in range(2):
        lanes = slice(t * 512, min(896, (t + 1) * 512))
        shares[2, :, lanes] = dot_nt(cot[rows, :], wd[lanes, :])
    shares_bf[2] = shares[2].astype(BF)
    sum_copies = {2: share(2)}

    rows = spread_res.group()
    for slot, weight in ((0, wg), (1, wu)):
        shares[slot] = dot(res[rows, :], weight[...])
        shares_bf[slot] = shares[slot].astype(BF)
        sum_copies[slot] = share(slot)

    spread_cot.forward()
    quarter = pl.ds(pl.multiple_of(me.y * 32, 32), 32)

    def total_of(slot):
        total = shares[slot, quarter, :]
        for k in range(me.tall - 1):
            sum_copies[slot][k].wait_recv()
            total = total + gathered[k, slot].astype(F32)
        return total

    hidden_grad = total_of(2)
    gate_sum = total_of(0)
    sigmoid = 1.0 / (1.0 + jnp.exp(-gate_sum))
    slope = hidden_grad * sigmoid * (1.0 + gate_sum * (1.0 - sigmoid))
    swish = gate_sum * sigmoid
    up_sum = total_of(1)
    spot_rows = pl.ds(pl.multiple_of(me.dp * 128 + me.y * 32, 32), 32)
    mid[1, spot_rows, :] = (slope * up_sum).astype(BF)
    mid[2, spot_rows, :] = (hidden_grad * swish).astype(BF)
    spot = mid.at[pl.ds(1, 2), spot_rows, :]
    mid_deltas = [send(spot, spot, sem_mid, k - 1, me.at_y(k)) for k in range(1, me.tall)]
    mid[0, spot_rows, :] = (swish * up_sum).astype(BF)
    spot = mid.at[0, spot_rows, :]
    mid_hidden = [send(spot, spot, sem_mid, 2 + k, me.at_y(k)) for k in range(1, me.tall)]
    spot = mid.at[:, spot_rows, :]
    mid_across = send(spot, spot, sem_mid, 6, me.across())
    spread_res.forward()
    for copy in mid_deltas:
        copy.wait_recv()

    rows = pl.ds(pl.multiple_of(me.dp * 128, 128), 128)
    for t in range(4):
        lanes = slice(t * 512, (t + 1) * 512)
        backs[0, :, lanes] = (
            dot_nt(mid[1, rows, :], wg[lanes, :]) + dot_nt(mid[2, rows, :], wu[lanes, :])
        ).astype(BF)
    backward = collect(backs.at[0], 1)
    backward.over_x()
    for copy in mid_hidden:
        copy.wait_recv()
    for t in range(2):
        lanes = slice(t * 1024, (t + 1) * 1024)
        backs[1, :, lanes] = dot(mid[0, rows, :], wd[:, lanes]).astype(BF)
    backward.over_z()
    forward = collect(backs.at[1], 2)
    forward.over_x()

    mid_across.wait_recv()
    spot = mid.at[:, pl.ds(pl.multiple_of(((me.dp + 2) % 4) * 128 + me.y * 32, 32), 32), :]
    mid_far = [send(spot, spot, sem_mid, 6 + k, me.at_y(k)) for k in range(1, me.tall)]
    spread_cot.over_cores()
    spread_res.over_cores()

    total = edge[1] + backward.total()
    spread_ig = Spread(me, ig, sem_ig)
    spread_ig.over_z(total.astype(BF))
    swap_ig = swap_out(me, total, swap_from.at[0], swap_to.at[0], sem_swap, 1)
    forward.over_z()
    spread_ig.over_x()

    for copy in mid_far:
        copy.wait_recv()
    mid_cores = []
    for k, dp in enumerate((me.dp, (me.dp + 2) % 4)):
        spot = mid.at[:, pl.ds(pl.multiple_of(dp * 128, 128), 128), :]
        mid_cores.append(send(spot, spot, sem_mid, 10 + k, me.sibling()))

    rows = spread_ig.group()
    near_sums[me.y] = dot_nt(ig[rows, :], wh[...]).astype(BF)
    spot = near_sums.at[me.y]
    cg_copies = [send(spot, spot, sem_cg, k - 1, me.at_y(k)) for k in range(1, me.tall)]
    spread_ig.forward()

    total = residual.astype(BF).astype(F32) + forward.total()
    swap_layer = swap_out(me, total, swap_from.at[1], swap_to.at[1], sem_swap, 2)
    ctx_copies[1].wait_recv()
    spot = ctx.at[pl.ds(pl.multiple_of(((me.dp + 2) % 4) * 128, 128), 128), :]
    ctx_copies.append(send(spot, spot, sem_ctx, 2, me.sibling()))
    swap_ig.wait_recv()
    input_grad[...] = swap_to[0].astype(BF)
    spread_ig.over_cores()

    for copy in cg_copies:
        copy.wait_recv()
    total = near_sums[0].astype(F32)
    for k in range(1, me.tall):
        total = total + near_sums[k].astype(F32)
    context_grad[...] = total.astype(BF)
    swap_layer.wait_recv()
    layer[...] = swap_to[1].astype(BF)

    for spread in (spread_cot, spread_res, spread_ig):
        spread.finish()
    for copy in mid_cores + [ctx_copies[0], ctx_copies[2]]:
        copy.wait_recv()
    for part in (spread_cot, spread_res, spread_ig, attention, backward, forward):
        part.drain()
    late = [entry, swap_ig, swap_layer, mid_across]
    late += ctx_copies + mid_deltas + mid_hidden + mid_far + mid_cores + cg_copies
    for slot in range(3):
        late += sum_copies[slot]
    for copy in late:
        copy.wait_send()


def chain_call(x8, cot8, context, lists, gate, up, down, heads):
    def sds(*shape):
        return jax.ShapeDtypeStruct(shape, BF)

    shapes = [
        sds(8, 2048), sds(8, 2048), sds(128, 256),
        sds(512, 2048), sds(512, 2048), sds(512, 2048), sds(3, 512, 896), sds(512, 256),
    ]
    dma = pltpu.SemaphoreType.DMA
    tall = lax.axis_size("in")
    depth = lax.axis_size("out") // 2
    return pl.pallas_call(
        chain_kernel,
        out_shape=shapes,
        in_specs=[VM] * 11 + [ANY] * 3 + [VM],
        out_specs=[VM] * 8,
        scratch_shapes=[
            pltpu.VMEM((240, CELL), BF),
            pltpu.VMEM((240, CELL), BF),
            pltpu.VMEM((240, CELL), BF),
            pltpu.VMEM((512, 2048), BF),
            pltpu.VMEM((2048, 896), BF),
            pltpu.VMEM((2048, 896), BF),
            pltpu.VMEM((896, 2048), BF),
            pltpu.VMEM((256, 2048), BF),
            pltpu.VMEM((128, 2048), BF),
            pltpu.VMEM((2, 8, 2048), F32),
            pltpu.VMEM((2, 16, 1024), F32),
            pltpu.VMEM((3, 128, 1024), BF),
            pltpu.VMEM((3, 128, 1024), BF),
            pltpu.VMEM((3, depth - 1, 16, 1024), BF),
            pltpu.VMEM((2, 128, 2048), BF),
            pltpu.VMEM((3, 128, 896), F32),
            pltpu.VMEM((3, 128, 896), BF),
            pltpu.VMEM((tall - 1, 3, 32, 896), BF),
            pltpu.VMEM((2, 16, 1024), F32),
            pltpu.VMEM((2, 8, 2048), F32),
            pltpu.VMEM((tall, 128, 256), BF),
            dma((3,)),
            dma((2, 21)),
            dma((2, 21)),
            dma((2, 21)),
            dma((3, 2, 16)),
            dma((2, 3)),
            dma((3, 2, 3)),
            dma((2, 12)),
            dma((2, 3)),
            dma((2, 3)),
        ],
        compiler_params=pltpu.CompilerParams(
            collective_id=0, has_side_effects=True, vmem_limit_bytes=58 * 2**20
        ),
        name="chain",
    )(x8, cot8, context, *lists, gate, up, down, heads)


def local(
    inputs, context,
    gate_blocks, gate_ids, gate_count,
    up_blocks, up_ids, up_count,
    down_blocks, down_ids, down_count,
    heads_blocks, heads_ids, heads_count,
    cotangent,
):
    rows = lambda blocks: blocks.reshape(-1, CELL)
    line = lambda ids: ids.reshape(1, -1)
    lists = (
        line(gate_ids), gate_count, line(up_ids), up_count,
        line(down_ids), down_count, line(heads_ids), heads_count,
    )
    layer, input_grad, context_grad, res, cot, ig, mid, ctx = chain_call(
        inputs, cotangent, context, lists,
        rows(gate_blocks), rows(up_blocks), rows(down_blocks), rows(heads_blocks),
    )
    grads = grads_call(lists, res, cot, ig, mid, ctx)
    return (layer, input_grad, context_grad, *(g.reshape(1, 1, -1, CELL) for g in grads))


def solution(mesh):
    rows = P(("dp", "out"), "in")
    tall, wide = ("in", "out"), ("out", "in")

    def lists(axes):
        return P(*axes, None, None), P(*axes, None), P(*axes)

    return jax.shard_map(
        local,
        mesh=mesh,
        in_specs=(rows, P("dp", "out"), *lists(tall), *lists(tall), *lists(wide), *lists(wide), rows),
        out_specs=(
            rows,
            rows,
            P("dp", "out"),
            P(*tall, "dp", None),
            P(*tall, "dp", None),
            P(*wide, "dp", None),
            P(*wide, "dp", None),
        ),
        check_vma=False,
    )
```

time: 163 us -> 121 us (0.74)
  Pallas kernels: 147 us -> 114 us
  local copies, waits for them, and re-layouts: 6.16 us -> 1.87 us
  other arithmetic: 4.19 us -> 0 us
    pallas_call x3 -> x2, Pallas kernels: 147 us -> 114 us  [the longest x1 93.5 us: chain_call(): pl.pallas_call(chain_kernel, out_shape=shapes, in_specs=[VM] * 11 + [ANY]...]
    squeeze x1 -> x0, local copies, waits for them, and re-layouts: 3.33 us -> none  [local(): grads = grads_call(idx, res, cot, ig, mid[0], mid[1], mid[2], ctx)]
where the time goes in v2:
time: 121 us; the launch traced here: 119 us
  Pallas kernels  114 us (94%)
  between operations  3.25 us (3%)
  local copies, waits for them, and re-layouts  1.87 us (2%)
    pallas_call x1, Pallas kernels, chain_call(): pl.pallas_call(chain_kernel, out_shape=shapes, in_specs=[VM] * 11 + [ANY]...  93.5 us
    pallas_call x1, Pallas kernels, grads_call(): pl.pallas_call(grads_kernel, out_shape=shapes, in_specs=[VM] * 13, out_sp...  20.7 us

profile of v2, /device:TPU:2, one launch (start us, length us, event | category | flops | bytes accessed | tf_op | source)
XLA Modules:
  0.0 119.3 jit_solution(17194823196959496002)
XLA Ops:
  3.2 93.5 %chain.1 = (bf16[8,2048]{1,0:T(8,128)(2,1)}, bf16[8,2048]{1,0:T(8,128)(2,1)}, bf16[128,256]{1,0:T(8,128)(2,1)}, bf16[512,2048]{1,0:T(8,128)(2,1)}, bf16[512,2048...) custom-call(bf16[8,2048]{1,0:T(8,128)(2,1)} %x8.1, ...), custom_call_target="tpu_custom_call" | custom-call | tf_op jit(solution)/shard_map/chain/pallas_call | solution.py:540
  96.7 0.0 copy-start.2
  96.7 0.0 copy-start.1
  96.7 0.0 copy-start
  96.7 20.7 %grads.1 = (bf16[60,4096]{1,0:T(8,128)(2,1)}, bf16[60,4096]{1,0:T(8,128)(2,1)}, bf16[60,4096]{1,0:T(8,128)(2,1)}, bf16[17,4096]{1,0:T(8,128)(2,1)}) custom-call(s32[1,240]{1,0:T(1,128)} %bitcast.17, s32[1,1]{1,0:T(1,128)S(6)} %copy.25.gcount, s32[1,240]{1,0:T(1,128)} %bitcast.19, s32[1,1]{1,0:T(1,128)S(6)} %copy.26.ucount, s32[1,240]{1,0:T(1,128)} %bitcast.21, ...), custom_call_target="tpu_custom_call" | custom-call | tf_op jit(solution)/shard_map/grads/pallas_call | solution.py:143
  117.4 0.0 copy-done.2
  117.4 0.6 copy.29
  118.0 0.0 copy-done.1
  118.0 0.6 copy.30
  118.6 0.0 copy-done
  118.6 0.6 copy.31
Async XLA Ops:
  96.7 20.7 %copy-start.2 = (bf16[8,2048]{1,0:T(8,128)(2,1)S(1)}, bf16[8,2048]{1,0:T(8,128)(2,1)}, u32[]{:S(2)}) copy-start(bf16[8,2048]{1,0:T(8,128)(2,1)} %get-tuple-element.38) | copy-start | bytes 98308
  96.7 21.3 %copy-start.1 = (bf16[8,2048]{1,0:T(8,128)(2,1)S(1)}, bf16[8,2048]{1,0:T(8,128)(2,1)}, u32[]{:S(2)}) copy-start(bf16[8,2048]{1,0:T(8,128)(2,1)} %get-tuple-element.39) | copy-start | bytes 98308
  96.7 21.9 %copy-start = (bf16[128,256]{1,0:T(8,128)(2,1)S(1)}, bf16[128,256]{1,0:T(8,128)(2,1)}, u32[]{:S(2)}) copy-start(bf16[128,256]{1,0:T(8,128)(2,1)} %get-tuple-element.40) | copy-start | bytes 196612

commit v3 on v2

--- a/solution.py
+++ b/solution.py
@@ -80,79 +80,89 @@
             out[at:at + chunk, :] = dense[r * chunk:(r + 1) * chunk]
 
 
-def pick(left, rights, hots, outs, flats, swap, turned, inner, used, stripes):
+def turn(left, turned, start, stop):
+    for s in range(start, stop):
+        turned[s * 128:(s + 1) * 128, :] = left[:, s * 128:(s + 1) * 128].T
+
+
+def order(turned, swap, ordered, inner, used, stripes, k):
     chunk = 256 // inner
-    span = used * BLOCK
-    for s in range(stripes * span // 128):
-        turned[s * 128:(s + 1) * 128, :] = left[:, s * 128:(s + 1) * 128].T
-
-    def step(k, _):
-        lanes = pl.ds(pl.multiple_of(k * chunk * BLOCK, chunk * BLOCK), chunk * BLOCK)
-        for s in range(stripes):
-            rows = [
-                turned[pl.ds(pl.multiple_of(s * span + r * BLOCK + k * chunk, 16), chunk), :]
-                for r in range(used)
-            ]
-            rows += [jnp.zeros_like(rows[0])] * (inner - used)
-            ordered = dot(swap, jnp.concatenate(rows, axis=0)).astype(BF)
-            for right, flat in zip(rights, flats):
-                width = right.shape[1]
-                base = s * (width // BLOCK) * inner
-                piece = 512 if width % 512 == 0 else 896
-                for t in range(width // piece):
-                    grad = dot(ordered, right[:, t * piece:(t + 1) * piece])
-                    for q in range(piece // 128):
-                        for p in range(chunk // 2):
-                            pair = grad[2 * p * inner:(2 * p + 2) * inner, q * 128:(q + 1) * 128]
-                            both = jnp.concatenate(halves(pair[:inner], pair[inner:]), axis=0)
-                            at = base + (t * piece // 128 + q) * 2 * inner
-                            flat[at:at + 2 * inner, p * 128:(p + 1) * 128] = both.astype(BF)
-        for hot, flat, out in zip(hots, flats, outs):
-            depth = hot.shape[0]
-            picked = dot_tn(hot, flat[:depth, :chunk * BLOCK])
-            out[:, lanes] = picked.astype(BF)
-        return 0
-
-    lax.fori_loop(0, BLOCK // chunk, step, 0)
-
-
-def grads_kernel(
-    gids, gcount, uids, ucount, dids, dcount, hids, hcount, res, cot, ig, mid, ctx,
-    og, ou, od, oh, turned, flat_a, flat_b,
+    for s in range(stripes):
+        rows = [
+            turned[s * used * BLOCK + r * BLOCK + k * chunk:s * used * BLOCK + r * BLOCK + (k + 1) * chunk, :]
+            for r in range(used)
+        ]
+        rows += [jnp.zeros_like(rows[0])] * (inner - used)
+        ordered[s * 256:(s + 1) * 256, :] = dot(swap, jnp.concatenate(rows, axis=0)).astype(BF)
+
+
+def pick(ordered, right, hot, out, flat, inner, stripes, k):
+    chunk = 256 // inner
+    width = right.shape[1]
+    piece = 1024 if width % 1024 == 0 else width
+    for s in range(stripes):
+        base = s * (width // BLOCK) * inner
+        for t in range(width // piece):
+            grad = dot(ordered[s * 256:(s + 1) * 256, :], right[:, t * piece:(t + 1) * piece]).astype(BF)
+            for q in range(piece // 128):
+                for p in range(chunk // 2):
+                    pair = grad[2 * p * inner:(2 * p + 2) * inner, q * 128:(q + 1) * 128]
+                    both = jnp.concatenate(halves(pair[:inner], pair[inner:]), axis=0)
+                    at = base + (t * piece // 128 + q) * 2 * inner
+                    flat[at:at + 2 * inner, p * 128:(p + 1) * 128] = both
+    picked = dot_tn(hot, flat[:hot.shape[0], :chunk * BLOCK])
+    out[:, k * chunk * BLOCK:(k + 1) * chunk * BLOCK] = picked.astype(BF)
+
+
+def own_hot(ids, count, kind, positions, share, slots, dp):
+    spot = spots(ids, count, kind)
+    if slots > share:
+        spot = jnp.concatenate([spot, jnp.full((1, slots - share), -1, jnp.int32)], axis=1)
+    own = spot[:, :slots]
+    for k in range(1, 4):
+        own = jnp.where(dp == k, spot[:, k * share:k * share + slots], own)
+    lanes = lax.broadcasted_iota(jnp.int32, own.shape, 1)
+    return one_hot(jnp.where(lanes < share, own, -1), positions)
+
+
+def finish_kernel(
+    hids, hcount, ctx, ig, layer, input_grad, context_grad, og, ou, od,
+    layer_to, input_grad_to, context_grad_to, og_to, ou_to, od_to, oh, turned, ordered, flat, sems,
 ):
-    swap16 = swap_matrix(16, 16)
-    dp = lax.axis_index("dp")
-
-    def hot(ids, count, kind, positions, share):
-        spot = spots(ids, count, kind)
-        own = spot[:, :share]
-        for k in range(1, 4):
-            own = jnp.where(dp == k, spot[:, k * share:(k + 1) * share], own)
-        return one_hot(own, positions)
-
-    hots = (hot(gids, gcount, "tall", 448, 60), hot(uids, ucount, "tall", 448, 60))
-    pick(res, (mid.at[1], mid.at[2]), hots, (og, ou), (flat_a, flat_b), swap16, turned, 16, 16, 2)
-    hots = (hot(dids, dcount, "wide", 512, 60),)
-    pick(mid.at[0], (cot,), hots, (od,), (flat_a,), swap16, turned, 16, 14, 1)
-    hots = (hot(hids, hcount, "heads", 256, 17),)
-    pick(ctx, (ig,), hots, (oh,), (flat_a,), swap_matrix(32, 8), turned, 8, 4, 1)
-
-
-def grads_call(lists, res, cot, ig, mid, ctx):
-    shapes = [jax.ShapeDtypeStruct((n, CELL), BF) for n in (60, 60, 60, 17)]
+    copies = []
+    pairs = ((og, og_to), (ou, ou_to), (od, od_to), (layer, layer_to), (input_grad, input_grad_to))
+    for k, (source, target) in enumerate(pairs + ((context_grad, context_grad_to),)):
+        if source.shape != target.shape:
+            source = source.at[:target.shape[0], :]
+        copies.append(pltpu.make_async_copy(source, target, sems.at[k]))
+        copies[-1].start()
+    hot = own_hot(hids, hcount, "heads", 256, 17, 17, lax.axis_index("dp"))
+    swap = swap_matrix(32, 8)
+    turn(ctx, turned, 0, 2)
+    for k in range(2):
+        order(turned, swap, ordered, 8, 4, 1, k)
+        pick(ordered, ig, hot, oh, flat, 8, 1, k)
+    for copy in copies:
+        copy.wait()
+
+
+def finish_call(hids, hcount, ctx, ig, *results):
+    shapes = [jax.ShapeDtypeStruct(r.shape, BF) for r in results]
+    shapes.append(jax.ShapeDtypeStruct((17, CELL), BF))
     return pl.pallas_call(
-        grads_kernel,
+        finish_kernel,
         out_shape=shapes,
-        in_specs=[VM] * 13,
-        out_specs=[VM] * 4,
+        in_specs=[VM] * 4 + [ANY] * 6,
+        out_specs=[ANY] * 6 + [VM],
         scratch_shapes=[
-            pltpu.VMEM((2048, 512), BF),
-            pltpu.VMEM((512, 2048), BF),
-            pltpu.VMEM((512, 2048), BF),
+            pltpu.VMEM((256, 512), BF),
+            pltpu.VMEM((256, 512), BF),
+            pltpu.VMEM((256, 2048), BF),
+            pltpu.SemaphoreType.DMA((6,)),
         ],
         compiler_params=pltpu.CompilerParams(vmem_limit_bytes=56 * 2**20),
-        name="grads",
-    )(*lists, res, cot, ig, mid, ctx)
+        name="finish",
+    )(hids, hcount, ctx, ig, *results)
 
 
 class Links:
@@ -238,10 +248,12 @@
         self.whole[self.chunk(me.z), self.home] = own
         self.first = {k: self.move(self.chunk(me.z), self.home, k, me.at_z(k)) for k in range(1, me.depth)}
 
-    def over_x(self):
+    def over_x(self, between=None):
         me, depth = self.me, self.me.depth
         self.near = [self.move(self.chunk(me.z), self.home, 8, me.beside())]
         for k in sorted(range(1, depth), key=lambda k: min(k, depth - k)):
+            if between is not None and k < depth - k + 1:
+                between(1)
             self.first[k].wait_recv()
             self.near.append(self.move(self.chunk(me.z + depth - k), self.home, 8 + k, me.beside()))
         self.wide = self.move(self.rows(me.dp), self.home, 16, self.far)
@@ -324,8 +336,8 @@
 
 def chain_kernel(
     x8, cot8, context, gids, gcount, uids, ucount, dids, dcount, hids, hcount, gate, up, down, heads,
-    layer, input_grad, context_grad, res, cot, ig, mid, ctx,
-    gate_in, up_in, down_in, stage, wg, wu, wd, wh, term,
+    layer, input_grad, context_grad, og, ou, od, ig, ctx,
+    res, cot, mid, turned, ordered, flat, gate_in, up_in, down_in, stage, wg, wu, wd, wh, term,
     cells, edge, halves_in, sums, parts, backs,
     shares, shares_bf, gathered, swap_from, swap_to, near_sums,
     sem_in, sem_res, sem_cot, sem_ig, sem_rs, sem_ctx, sem_sum, sem_mid, sem_cg, sem_swap,
@@ -459,6 +471,10 @@
         ).astype(BF)
     backward = collect(backs.at[0], 1)
     backward.over_x()
+
+    mid_across.wait_recv()
+    spot = mid.at[:, pl.ds(pl.multiple_of(((me.dp + 2) % 4) * 128 + me.y * 32, 32), 32), :]
+    mid_far = [send(spot, spot, sem_mid, 6 + k, me.at_y(k)) for k in range(1, me.tall)]
     for copy in mid_hidden:
         copy.wait_recv()
     for t in range(2):
@@ -467,19 +483,31 @@
     backward.over_z()
     forward = collect(backs.at[1], 2)
     forward.over_x()
-
-    mid_across.wait_recv()
-    spot = mid.at[:, pl.ds(pl.multiple_of(((me.dp + 2) % 4) * 128 + me.y * 32, 32), 32), :]
-    mid_far = [send(spot, spot, sem_mid, 6 + k, me.at_y(k)) for k in range(1, me.tall)]
+    spread_res.over_cores()
     spread_cot.over_cores()
-    spread_res.over_cores()
-
-    total = edge[1] + backward.total()
-    spread_ig = Spread(me, ig, sem_ig)
-    spread_ig.over_z(total.astype(BF))
-    swap_ig = swap_out(me, total, swap_from.at[0], swap_to.at[0], sem_swap, 1)
-    forward.over_z()
-    spread_ig.over_x()
+
+    held = {}
+
+    def pick_tall(k, slot, out):
+        if slot == 1:
+            order(turned, swap16, ordered, 16, 16, 2, k)
+        if slot not in held:
+            ids, count = ((gids, gcount), (uids, ucount))[slot - 1]
+            held[slot] = own_hot(ids, count, "tall", 448, 60, 60, me.dp)
+        pick(ordered, mid.at[slot], held[slot], out, flat, 16, 2, k)
+
+    def pick_wide(k):
+        if k == 0:
+            turn(mid.at[0], turned, 0, 7)
+            held[0] = own_hot(dids, dcount, "wide", 512, 60, 60, me.dp)
+        order(turned, swap16, ordered, 16, 14, 1, k)
+        pick(ordered, cot, held[0], od, flat, 16, 1, k)
+
+    for k in range(4):
+        work.append(lambda k=k: pick_tall(k, 1, og))
+        work.append(lambda k=k: pick_tall(k, 2, ou))
+    for k in range(4):
+        work.append(lambda k=k: pick_wide(k))
 
     for copy in mid_far:
         copy.wait_recv()
@@ -487,21 +515,37 @@
     for k, dp in enumerate((me.dp, (me.dp + 2) % 4)):
         spot = mid.at[:, pl.ds(pl.multiple_of(dp * 128, 128), 128), :]
         mid_cores.append(send(spot, spot, sem_mid, 10 + k, me.sibling()))
+    spread_res.finish()
+    turn(res, turned, 0, 16)
+
+    total = edge[1] + backward.total()
+    spread_ig = Spread(me, ig, sem_ig)
+    spread_ig.over_z(total.astype(BF))
+    swap_ig = swap_out(me, total, swap_from.at[0], swap_to.at[0], sem_swap, 1)
+    for copy in mid_cores:
+        copy.wait_recv()
+    spread_cot.finish()
+    fill(1)
+    spread_ig.over_x(fill)
+    forward.over_z()
+    fill(1)
 
     rows = spread_ig.group()
     near_sums[me.y] = dot_nt(ig[rows, :], wh[...]).astype(BF)
     spot = near_sums.at[me.y]
     cg_copies = [send(spot, spot, sem_cg, k - 1, me.at_y(k)) for k in range(1, me.tall)]
     spread_ig.forward()
+    fill(2)
+    spread_ig.over_cores()
 
     total = residual.astype(BF).astype(F32) + forward.total()
     swap_layer = swap_out(me, total, swap_from.at[1], swap_to.at[1], sem_swap, 2)
     ctx_copies[1].wait_recv()
     spot = ctx.at[pl.ds(pl.multiple_of(((me.dp + 2) % 4) * 128, 128), 128), :]
     ctx_copies.append(send(spot, spot, sem_ctx, 2, me.sibling()))
+    fill(len(work))
     swap_ig.wait_recv()
     input_grad[...] = swap_to[0].astype(BF)
-    spread_ig.over_cores()
 
     for copy in cg_copies:
         copy.wait_recv()
@@ -512,9 +556,8 @@
     swap_layer.wait_recv()
     layer[...] = swap_to[1].astype(BF)
 
-    for spread in (spread_cot, spread_res, spread_ig):
-        spread.finish()
-    for copy in mid_cores + [ctx_copies[0], ctx_copies[2]]:
+    spread_ig.finish()
+    for copy in [ctx_copies[0], ctx_copies[2]]:
         copy.wait_recv()
     for part in (spread_cot, spread_res, spread_ig, attention, backward, forward):
         part.drain()
@@ -532,7 +575,7 @@
 
     shapes = [
         sds(8, 2048), sds(8, 2048), sds(128, 256),
-        sds(512, 2048), sds(512, 2048), sds(512, 2048), sds(3, 512, 896), sds(512, 256),
+        sds(60, CELL), sds(60, CELL), sds(60, CELL), sds(512, 2048), sds(512, 256),
     ]
     dma = pltpu.SemaphoreType.DMA
     tall = lax.axis_size("in")
@@ -543,6 +586,12 @@
         in_specs=[VM] * 11 + [ANY] * 3 + [VM],
         out_specs=[VM] * 8,
         scratch_shapes=[
+            pltpu.VMEM((512, 2048), BF),
+            pltpu.VMEM((512, 2048), BF),
+            pltpu.VMEM((3, 512, 896), BF),
+            pltpu.VMEM((2048, 512), BF),
+            pltpu.VMEM((512, 512), BF),
+            pltpu.VMEM((512, 1024), BF),
             pltpu.VMEM((240, CELL), BF),
             pltpu.VMEM((240, CELL), BF),
             pltpu.VMEM((240, CELL), BF),
@@ -596,12 +645,12 @@
         line(gate_ids), gate_count, line(up_ids), up_count,
         line(down_ids), down_count, line(heads_ids), heads_count,
     )
-    layer, input_grad, context_grad, res, cot, ig, mid, ctx = chain_call(
+    *results, ig, ctx = chain_call(
         inputs, cotangent, context, lists,
         rows(gate_blocks), rows(up_blocks), rows(down_blocks), rows(heads_blocks),
     )
-    grads = grads_call(lists, res, cot, ig, mid, ctx)
-    return (layer, input_grad, context_grad, *(g.reshape(1, 1, -1, CELL) for g in grads))
+    *done, og, ou, od, oh = finish_call(line(heads_ids), heads_count, ctx, ig, *results)
+    return (*done, *(g.reshape(1, 1, -1, CELL) for g in (og, ou, od, oh)))
 
 
 def solution(mesh):

time: 121 us -> 157 us (1.30)
  Pallas kernels: 114 us -> 153 us
  local copies, waits for them, and re-layouts: 1.87 us -> 0 us
    pallas_call x1, Pallas kernels: 20.7 us -> 55.1 us  [finish_call(): pl.pallas_call(finish_kernel, out_shape=shapes, in_specs=[VM] * 4 + [ANY]...]
    pallas_call x1, Pallas kernels: 93.5 us -> 98 us  [chain_call(): pl.pallas_call(chain_kernel, out_shape=shapes, in_specs=[VM] * 11 + [ANY]...]
    unnamed x9 -> x0, local copies, waits for them, and re-layouts: 1.87 us -> none
where the time goes in v3:
time: 157 us
  Pallas kernels  153 us (97%)
  between operations  3.41 us (2%)
    pallas_call x1, Pallas kernels, chain_call(): pl.pallas_call(chain_kernel, out_shape=shapes, in_specs=[VM] * 11 + [ANY]...  98 us
    pallas_call x1, Pallas kernels, finish_call(): pl.pallas_call(finish_kernel, out_shape=shapes, in_specs=[VM] * 4 + [ANY]...  55.1 us

profile of v3, /device:TPU:2, one launch (start us, length us, event | category | flops | bytes accessed | tf_op | source)
XLA Modules:
  0.0 156.5 jit_solution(5630061195495022411)
XLA Ops:
  3.2 98.0 %chain.1 = (bf16[8,2048]{1,0:T(8,128)(2,1)}, bf16[8,2048]{1,0:T(8,128)(2,1)}, bf16[128,256]{1,0:T(8,128)(2,1)}, bf16[60,4096]{1,0:T(8,128)(2,1)}, bf16[60,4096]{...) custom-call(bf16[8,2048]{1,0:T(8,128)(2,1)} %x8.1, ...), custom_call_target="tpu_custom_call" | custom-call | tf_op jit(solution)/shard_map/chain/pallas_call | solution.py:583
  101.2 55.1 %finish.1 = (bf16[8,2048]{1,0:T(8,128)(2,1)}, bf16[8,2048]{1,0:T(8,128)(2,1)}, bf16[128,256]{1,0:T(8,128)(2,1)}, bf16[60,4096]{1,0:T(8,128)(2,1)}, bf16[60,4096]...) custom-call(s32[1,68]{1,0:T(1,128)} %bitcast.17, s32[1,1]{1,0:T(1,128)S(6)} %copy.25.hcount, ...), custom_call_target="tpu_custom_call" | custom-call | tf_op jit(solution)/shard_map/finish/pallas_call | solution.py:152

commit v4 on v3

--- a/solution.py
+++ b/solution.py
@@ -125,44 +125,25 @@
     return one_hot(jnp.where(lanes < share, own, -1), positions)
 
 
-def finish_kernel(
-    hids, hcount, ctx, ig, layer, input_grad, context_grad, og, ou, od,
-    layer_to, input_grad_to, context_grad_to, og_to, ou_to, od_to, oh, turned, ordered, flat, sems,
-):
-    copies = []
-    pairs = ((og, og_to), (ou, ou_to), (od, od_to), (layer, layer_to), (input_grad, input_grad_to))
-    for k, (source, target) in enumerate(pairs + ((context_grad, context_grad_to),)):
-        if source.shape != target.shape:
-            source = source.at[:target.shape[0], :]
-        copies.append(pltpu.make_async_copy(source, target, sems.at[k]))
-        copies[-1].start()
-    hot = own_hot(hids, hcount, "heads", 256, 17, 17, lax.axis_index("dp"))
-    swap = swap_matrix(32, 8)
-    turn(ctx, turned, 0, 2)
-    for k in range(2):
-        order(turned, swap, ordered, 8, 4, 1, k)
-        pick(ordered, ig, hot, oh, flat, 8, 1, k)
+def finish_kernel(*refs):
+    count = (len(refs) - 1) // 2
+    copies = [pltpu.make_async_copy(refs[k], refs[count + k], refs[-1].at[k]) for k in range(count)]
+    for copy in copies:
+        copy.start()
     for copy in copies:
         copy.wait()
 
 
-def finish_call(hids, hcount, ctx, ig, *results):
-    shapes = [jax.ShapeDtypeStruct(r.shape, BF) for r in results]
-    shapes.append(jax.ShapeDtypeStruct((17, CELL), BF))
+def finish_call(*results):
     return pl.pallas_call(
         finish_kernel,
-        out_shape=shapes,
-        in_specs=[VM] * 4 + [ANY] * 6,
-        out_specs=[ANY] * 6 + [VM],
-        scratch_shapes=[
-            pltpu.VMEM((256, 512), BF),
-            pltpu.VMEM((256, 512), BF),
-            pltpu.VMEM((256, 2048), BF),
-            pltpu.SemaphoreType.DMA((6,)),
-        ],
-        compiler_params=pltpu.CompilerParams(vmem_limit_bytes=56 * 2**20),
+        out_shape=[jax.ShapeDtypeStruct(r.shape, BF) for r in results],
+        in_specs=[VM] * len(results),
+        out_specs=[ANY] * len(results),
+        scratch_shapes=[pltpu.SemaphoreType.DMA((len(results),))],
+        compiler_params=pltpu.CompilerParams(vmem_limit_bytes=16 * 2**20),
         name="finish",
-    )(hids, hcount, ctx, ig, *results)
+    )(*results)
 
 
 class Links:
@@ -223,13 +204,13 @@
 
 class Spread:
 
-    def __init__(self, me, whole, sems):
-        self.me, self.whole, self.sems = me, whole, sems
+    def __init__(self, me, whole, sems, splits=1):
+        self.me, self.whole, self.sems, self.width = me, whole, sems, 1024 // splits
         self.home = pl.ds(pl.multiple_of(me.low * 1024, 1024), 1024)
         self.away = pl.ds(pl.multiple_of((1 - me.low) * 1024, 1024), 1024)
         self.other = (me.dp + 2) % 4
         self.far = me.at_x(jnp.where(me.low == 0, 3, 1))
-        self.sent = []
+        self.sent, self.first, self.near = [], {}, []
 
     def rows(self, dp, start=0, size=128):
         return pl.ds(pl.multiple_of(dp * 128 + start, 16), size)
@@ -243,20 +224,29 @@
     def chunk(self, z):
         return pl.ds(pl.multiple_of(self.me.dp * 128 + (z % self.me.depth) * 16, 16), 16)
 
-    def over_z(self, own):
+    def part(self, h):
+        return pl.ds(pl.multiple_of(self.me.low * 1024 + h * self.width, self.width), self.width)
+
+    def over_z(self, own, h=0):
         me = self.me
-        self.whole[self.chunk(me.z), self.home] = own
-        self.first = {k: self.move(self.chunk(me.z), self.home, k, me.at_z(k)) for k in range(1, me.depth)}
-
-    def over_x(self, between=None):
+        self.whole[self.chunk(me.z), self.part(h)] = own
+        ks = sorted(range(1, me.depth), key=lambda k: -min(k, me.depth - k))
+        self.first[h] = {
+            k: self.move(self.chunk(me.z), self.part(h), h * 8 + k, me.at_z(k)) for k in ks
+        }
+
+    def over_x(self, between=None, h=0):
         me, depth = self.me, self.me.depth
-        self.near = [self.move(self.chunk(me.z), self.home, 8, me.beside())]
+        at = 16 + h * 8
+        self.near.append(self.move(self.chunk(me.z), self.part(h), at, me.beside()))
         for k in sorted(range(1, depth), key=lambda k: min(k, depth - k)):
             if between is not None and k < depth - k + 1:
                 between(1)
-            self.first[k].wait_recv()
-            self.near.append(self.move(self.chunk(me.z + depth - k), self.home, 8 + k, me.beside()))
-        self.wide = self.move(self.rows(me.dp), self.home, 16, self.far)
+            self.first[h][k].wait_recv()
+            self.near.append(self.move(self.chunk(me.z + depth - k), self.part(h), at + k, me.beside()))
+
+    def widen(self):
+        self.wide = self.move(self.rows(self.me.dp), self.home, 32, self.far)
 
     def group(self):
         for copy in self.near:
@@ -265,15 +255,15 @@
 
     def forward(self):
         me = self.me
-        self.half_a = self.move(self.rows(me.dp, 0, 64), self.away, 17, self.far)
-        self.cores = [self.move(self.rows(me.dp), slice(None), 19, me.sibling())]
+        self.half_a = self.move(self.rows(me.dp, 0, 64), self.away, 33, self.far)
+        self.cores = [self.move(self.rows(me.dp), slice(None), 35, me.sibling())]
         self.wide.wait_recv()
-        self.half_b = self.move(self.rows(self.other, 64, 64), self.away, 18, me.beside())
+        self.half_b = self.move(self.rows(self.other, 64, 64), self.away, 34, me.beside())
 
     def over_cores(self):
         self.half_a.wait_recv()
         self.half_b.wait_recv()
-        self.cores.append(self.move(self.rows(self.other), slice(None), 20, self.me.sibling()))
+        self.cores.append(self.move(self.rows(self.other), slice(None), 36, self.me.sibling()))
 
     def finish(self):
         for copy in self.cores:
@@ -286,39 +276,45 @@
 
 class Collect:
 
-    def __init__(self, me, term, half, sums, parts, sems):
+    def __init__(self, me, term, half, sums, parts, sems, splits=1):
         self.me, self.term, self.half, self.sums, self.parts, self.sems = me, term, half, sums, parts, sems
+        self.width = 1024 // splits
         self.order = sorted(range(me.depth), key=lambda k: -min(k, me.depth - k))
+        self.near, self.far, self.own = {}, {}, {}
 
     def chunk(self, k):
         return pl.ds(pl.multiple_of(((self.me.z + k) % self.me.depth) * 16, 16), 16)
 
-    def over_x(self):
-        away = pl.ds(pl.multiple_of((1 - self.me.low) * 1024, 1024), 1024)
-        self.near = {}
+    def lanes(self, h, low=0):
+        return pl.ds(pl.multiple_of(low * 1024 + h * self.width, self.width), self.width)
+
+    def over_x(self, h=0):
         for k in self.order:
             rows = self.chunk(k)
-            self.near[k] = send(self.term.at[rows, away], self.half.at[rows, :], self.sems, 8 + k, self.me.beside())
-
-    def over_z(self):
-        me = self.me
-        home = pl.ds(pl.multiple_of(me.low * 1024, 1024), 1024)
-        self.far = {}
+            self.near[h, k] = send(
+                self.term.at[rows, self.lanes(h, 1 - self.me.low)], self.half.at[rows, self.lanes(h)],
+                self.sems, h * 8 + k, self.me.beside(),
+            )
+
+    def over_z(self, h=0):
+        me, lanes = self.me, self.lanes(h)
         for k in self.order:
             rows = self.chunk(k)
-            self.near[k].wait_recv()
-            both = self.term[rows, home].astype(F32) + self.half[rows, :].astype(F32)
+            self.near[h, k].wait_recv()
+            both = self.term[rows, self.lanes(h, me.low)].astype(F32) + self.half[rows, lanes].astype(F32)
             if k == 0:
-                self.own = both
+                self.own[h] = both
             else:
-                self.sums[rows, :] = both.astype(BF)
-                self.far[k] = send(self.sums.at[rows, :], self.parts.at[k - 1], self.sems, k, me.at_z(k))
-
-    def total(self):
-        total = self.own
+                self.sums[rows, lanes] = both.astype(BF)
+                self.far[h, k] = send(
+                    self.sums.at[rows, lanes], self.parts.at[k - 1, :, lanes], self.sems, 16 + h * 8 + k, me.at_z(k)
+                )
+
+    def total(self, h=0):
+        total = self.own[h]
         for k in reversed(self.order[:-1]):
-            self.far[k].wait_recv()
-            total = total + self.parts[k - 1].astype(F32)
+            self.far[h, k].wait_recv()
+            total = total + self.parts[k - 1, :, self.lanes(h)].astype(F32)
         return total
 
     def drain(self):
@@ -326,8 +322,7 @@
             copy.wait_send()
 
 
-def swap_out(me, total, outgoing, landing, sems, k):
-    outgoing[...] = total
+def swap_out(me, outgoing, landing, sems, k):
     away = outgoing.at[pl.ds(pl.multiple_of((1 - me.low) * 8, 8), 8), :]
     lanes = pl.ds(pl.multiple_of(me.low * 1024, 1024), 1024)
     landing[:, lanes] = outgoing[pl.ds(pl.multiple_of(me.low * 8, 8), 8), :]
@@ -336,8 +331,8 @@
 
 def chain_kernel(
     x8, cot8, context, gids, gcount, uids, ucount, dids, dcount, hids, hcount, gate, up, down, heads,
-    layer, input_grad, context_grad, og, ou, od, ig, ctx,
-    res, cot, mid, turned, ordered, flat, gate_in, up_in, down_in, stage, wg, wu, wd, wh, term,
+    layer, input_grad, context_grad, og, ou, od, oh,
+    ig, ctx, res, cot, mid, turned, ordered, flat, gate_in, up_in, down_in, stage, wg, wu, wd, wh, term,
     cells, edge, halves_in, sums, parts, backs,
     shares, shares_bf, gathered, swap_from, swap_to, near_sums,
     sem_in, sem_res, sem_cot, sem_ig, sem_rs, sem_ctx, sem_sum, sem_mid, sem_cg, sem_swap,
@@ -384,17 +379,20 @@
     home = pl.ds(pl.multiple_of(me.low * 1024, 1024), 1024)
 
     def collect(term, k):
-        return Collect(me, term, halves_in.at[k], sums.at[k], parts.at[k], sem_rs.at[k])
+        return Collect(me, term, halves_in.at[k], sums.at[k], parts.at[k], sem_rs.at[k], 1 if k == 2 else 2)
 
     cells[0] = x8[...].astype(F32)
     cells[1] = cot8[...].astype(F32)
     edge[:, low8, :] = cells[:, :, home]
     me.meet(greeted)
     attention = collect(term, 0)
-    attention.over_x()
+    attention.over_x(0)
     entry = send(cells.at[:, :, away], edge.at[:, low8, :], sem_swap, 0, me.beside())
-    fill(3)
-    attention.over_z()
+    attention.over_x(1)
+    fill(2)
+    attention.over_z(0)
+    fill(1)
+    attention.over_z(1)
     entry.wait_recv()
     spread_cot = Spread(me, cot, sem_cot)
     spread_cot.over_z(edge[1].astype(BF))
@@ -402,14 +400,20 @@
     ctx[own_ctx, :] = context[...]
     spot = ctx.at[own_ctx, :]
     ctx_copies = [send(spot, spot, sem_ctx, k, to) for k, to in enumerate((me.sibling(), me.across()))]
+    fill(2)
+    spread_res = Spread(me, res, sem_res, 2)
+    for h in range(2):
+        cols = slice(h * 512, (h + 1) * 512)
+        spread_res.over_z((edge[0, :, cols] + attention.total(h)).astype(BF), h)
+        fill(1)
+    spread_cot.over_x()
+    spread_cot.widen()
+    fill(1)
+    spread_res.over_x(None, 0)
+    fill(1)
+    spread_res.over_x(None, 1)
+    spread_res.widen()
     fill(3)
-    residual = edge[0] + attention.total()
-    spread_res = Spread(me, res, sem_res)
-    spread_res.over_z(residual.astype(BF))
-    spread_cot.over_x()
-    fill(2)
-    spread_res.over_x()
-    fill(4)
 
     def share(slot):
         copies = []
@@ -470,7 +474,8 @@
             dot_nt(mid[1, rows, :], wg[lanes, :]) + dot_nt(mid[2, rows, :], wu[lanes, :])
         ).astype(BF)
     backward = collect(backs.at[0], 1)
-    backward.over_x()
+    backward.over_x(0)
+    backward.over_x(1)
 
     mid_across.wait_recv()
     spot = mid.at[:, pl.ds(pl.multiple_of(((me.dp + 2) % 4) * 128 + me.y * 32, 32), 32), :]
@@ -480,7 +485,8 @@
     for t in range(2):
         lanes = slice(t * 1024, (t + 1) * 1024)
         backs[1, :, lanes] = dot(mid[0, rows, :], wd[:, lanes]).astype(BF)
-    backward.over_z()
+    backward.over_z(0)
+    backward.over_z(1)
     forward = collect(backs.at[1], 2)
     forward.over_x()
     spread_res.over_cores()
@@ -518,15 +524,20 @@
     spread_res.finish()
     turn(res, turned, 0, 16)
 
-    total = edge[1] + backward.total()
-    spread_ig = Spread(me, ig, sem_ig)
-    spread_ig.over_z(total.astype(BF))
-    swap_ig = swap_out(me, total, swap_from.at[0], swap_to.at[0], sem_swap, 1)
+    spread_ig = Spread(me, ig, sem_ig, 2)
+    for h in range(2):
+        cols = slice(h * 512, (h + 1) * 512)
+        total = edge[1, :, cols] + backward.total(h)
+        spread_ig.over_z(total.astype(BF), h)
+        swap_from[0, :, cols] = total
+    swap_ig = swap_out(me, swap_from.at[0], swap_to.at[0], sem_swap, 1)
     for copy in mid_cores:
         copy.wait_recv()
     spread_cot.finish()
     fill(1)
-    spread_ig.over_x(fill)
+    spread_ig.over_x(fill, 0)
+    spread_ig.over_x(None, 1)
+    spread_ig.widen()
     forward.over_z()
     fill(1)
 
@@ -538,8 +549,8 @@
     fill(2)
     spread_ig.over_cores()
 
-    total = residual.astype(BF).astype(F32) + forward.total()
-    swap_layer = swap_out(me, total, swap_from.at[1], swap_to.at[1], sem_swap, 2)
+    swap_from[1] = res[spread_res.chunk(me.z), home].astype(F32) + forward.total()
+    swap_layer = swap_out(me, swap_from.at[1], swap_to.at[1], sem_swap, 2)
     ctx_copies[1].wait_recv()
     spot = ctx.at[pl.ds(pl.multiple_of(((me.dp + 2) % 4) * 128, 128), 128), :]
     ctx_copies.append(send(spot, spot, sem_ctx, 2, me.sibling()))
@@ -556,9 +567,16 @@
     swap_layer.wait_recv()
     layer[...] = swap_to[1].astype(BF)
 
-    spread_ig.finish()
     for copy in [ctx_copies[0], ctx_copies[2]]:
         copy.wait_recv()
+    turn(ctx, turned, 0, 2)
+    swap = swap_matrix(32, 8)
+    hot = own_hot(hids, hcount, "heads", 256, 17, 17, me.dp)
+    for k in range(2):
+        order(turned, swap, ordered.at[pl.ds(k * 256, 256), :], 8, 4, 1, k)
+    spread_ig.finish()
+    for k in range(2):
+        pick(ordered.at[pl.ds(k * 256, 256), :], ig, hot, oh, flat, 8, 1, k)
     for part in (spread_cot, spread_res, spread_ig, attention, backward, forward):
         part.drain()
     late = [entry, swap_ig, swap_layer, mid_across]
@@ -575,7 +593,7 @@
 
     shapes = [
         sds(8, 2048), sds(8, 2048), sds(128, 256),
-        sds(60, CELL), sds(60, CELL), sds(60, CELL), sds(512, 2048), sds(512, 256),
+        sds(60, CELL), sds(60, CELL), sds(60, CELL), sds(17, CELL),
     ]
     dma = pltpu.SemaphoreType.DMA
     tall = lax.axis_size("in")
@@ -584,14 +602,16 @@
         chain_kernel,
         out_shape=shapes,
         in_specs=[VM] * 11 + [ANY] * 3 + [VM],
-        out_specs=[VM] * 8,
+        out_specs=[VM] * 7,
         scratch_shapes=[
+            pltpu.VMEM((512, 2048), BF),
+            pltpu.VMEM((512, 256), BF),
             pltpu.VMEM((512, 2048), BF),
             pltpu.VMEM((512, 2048), BF),
             pltpu.VMEM((3, 512, 896), BF),
             pltpu.VMEM((2048, 512), BF),
             pltpu.VMEM((512, 512), BF),
-            pltpu.VMEM((512, 1024), BF),
+            pltpu.VMEM((512, 2048), BF),
             pltpu.VMEM((240, CELL), BF),
             pltpu.VMEM((240, CELL), BF),
             pltpu.VMEM((240, CELL), BF),
@@ -614,10 +634,10 @@
             pltpu.VMEM((2, 8, 2048), F32),
             pltpu.VMEM((tall, 128, 256), BF),
             dma((3,)),
-            dma((2, 21)),
-            dma((2, 21)),
-            dma((2, 21)),
-            dma((3, 2, 16)),
+            dma((2, 37)),
+            dma((2, 37)),
+            dma((2, 37)),
+            dma((3, 2, 32)),
             dma((2, 3)),
             dma((3, 2, 3)),
             dma((2, 12)),
@@ -645,12 +665,12 @@
         line(gate_ids), gate_count, line(up_ids), up_count,
         line(down_ids), down_count, line(heads_ids), heads_count,
     )
-    *results, ig, ctx = chain_call(
+    results = chain_call(
         inputs, cotangent, context, lists,
         rows(gate_blocks), rows(up_blocks), rows(down_blocks), rows(heads_blocks),
     )
-    *done, og, ou, od, oh = finish_call(line(heads_ids), heads_count, ctx, ig, *results)
-    return (*done, *(g.reshape(1, 1, -1, CELL) for g in (og, ou, od, oh)))
+    done = finish_call(*results)
+    return (*done[:3], *(g.reshape(1, 1, -1, CELL) for g in done[3:]))
 
 
 def solution(mesh):

time: 157 us -> 110 us (0.70)
  Pallas kernels: 153 us -> 99.9 us
  local copies, waits for them, and re-layouts: 0 us -> 6.4 us
    pallas_call x1, Pallas kernels: 55.1 us -> 1.3 us  [finish_call(): pl.pallas_call(finish_kernel, out_shape=[jax.ShapeDtypeStruct(r.shape, BF...]
    unnamed x0 -> x14, local copies, waits for them, and re-layouts: none -> 6.4 us
where the time goes in v4:
time: 110 us
  Pallas kernels  99.9 us (91%)
  local copies, waits for them, and re-layouts  6.4 us (6%)
  between operations  3.42 us (3%)
    pallas_call x1, Pallas kernels, chain_call(): pl.pallas_call(chain_kernel, out_shape=shapes, in_specs=[VM] * 11 + [ANY]...  98.6 us
    unnamed x14, local copies, waits for them, and re-layouts  6.4 us

profile of v4, /device:TPU:2, one launch (start us, length us, event | category | flops | bytes accessed | tf_op | source)
XLA Modules:
  0.0 109.7 jit_solution(4971885454887909473)
XLA Ops:
  3.2 98.6 %chain.1 = (bf16[8,2048]{1,0:T(8,128)(2,1)}, bf16[8,2048]{1,0:T(8,128)(2,1)}, bf16[128,256]{1,0:T(8,128)(2,1)}, bf16[60,4096]{1,0:T(8,128)(2,1)}, bf16[60,4096]{...) custom-call(bf16[8,2048]{1,0:T(8,128)(2,1)} %x8.1, bf16[8,2048]{1,0:T(8,128)(2,1)} %cot8.1, ...), custom_call_target="tpu_custom_call" | custom-call | tf_op jit(solution)/shard_map/chain/pallas_call | solution.py:601
  101.8 0.0 copy-start
  101.8 1.0 copy-done
  102.9 0.0 copy-start.1
  102.9 1.0 copy-done.1
  103.9 0.0 copy-start.2
  103.9 1.0 copy-done.2
  105.0 0.0 copy-start.3
  105.0 0.9 copy-done.3
  105.9 0.0 copy-start.4
  105.9 0.8 copy-done.4
  106.7 0.0 copy-start.5
  106.7 0.8 copy-done.5
  107.5 0.0 copy-start.6
  107.5 0.8 copy-done.6
  108.2 1.3 %finish.1 = (bf16[8,2048]{1,0:T(8,128)(2,1)}, bf16[8,2048]{1,0:T(8,128)(2,1)}, bf16[128,256]{1,0:T(8,128)(2,1)}, bf16[60,4096]{1,0:T(8,128)(2,1)}, bf16[60,4096]...) custom-call(bf16[8,2048]{1,0:T(8,128)(2,1)S(1)} %copy-done.5, bf16[8,2048]{1,0:T(8,128)(2,1)S(1)} %copy-done.6, ...), custom_call_target="tpu_custom_call" | custom-call | tf_op jit(solution)/shard_map/finish/pallas_call | solution.py:138
Async XLA Ops:
  101.8 1.0 copy-start
  102.9 1.0 copy-start.1
  103.9 1.0 copy-start.2
  105.0 0.9 copy-start.3
  105.9 0.8 copy-start.4
  106.7 0.8 copy-start.5
  107.5 0.8 copy-start.6

commit v5 on v4

--- a/solution.py
+++ b/solution.py
@@ -126,11 +126,16 @@
 
 
 def finish_kernel(*refs):
-    count = (len(refs) - 1) // 2
-    copies = [pltpu.make_async_copy(refs[k], refs[count + k], refs[-1].at[k]) for k in range(count)]
-    for copy in copies:
+    count = (len(refs) - 1) // 3
+    sources, targets, held, sems = refs[:count], refs[count:2 * count], refs[2 * count:-1], refs[-1]
+    loads = [pltpu.make_async_copy(sources[k], held[k], sems.at[0, k]) for k in range(count)]
+    stores = [pltpu.make_async_copy(held[k], targets[k], sems.at[1, k]) for k in range(count)]
+    for copy in loads:
         copy.start()
-    for copy in copies:
+    for load, store in zip(loads, stores):
+        load.wait()
+        store.start()
+    for copy in stores:
         copy.wait()
 
 
@@ -138,10 +143,11 @@
     return pl.pallas_call(
         finish_kernel,
         out_shape=[jax.ShapeDtypeStruct(r.shape, BF) for r in results],
-        in_specs=[VM] * len(results),
+        in_specs=[ANY] * len(results),
         out_specs=[ANY] * len(results),
-        scratch_shapes=[pltpu.SemaphoreType.DMA((len(results),))],
-        compiler_params=pltpu.CompilerParams(vmem_limit_bytes=16 * 2**20),
+        scratch_shapes=[pltpu.VMEM(r.shape, BF) for r in results]
+        + [pltpu.SemaphoreType.DMA((2, len(results)))],
+        compiler_params=pltpu.CompilerParams(vmem_limit_bytes=58 * 2**20),
         name="finish",
     )(*results)
 
@@ -438,6 +444,7 @@
         sum_copies[slot] = share(slot)
 
     spread_cot.forward()
+    spread_res.forward()
     quarter = pl.ds(pl.multiple_of(me.y * 32, 32), 32)
 
     def total_of(slot):
@@ -463,34 +470,38 @@
     mid_hidden = [send(spot, spot, sem_mid, 2 + k, me.at_y(k)) for k in range(1, me.tall)]
     spot = mid.at[:, spot_rows, :]
     mid_across = send(spot, spot, sem_mid, 6, me.across())
-    spread_res.forward()
+    spread_res.over_cores()
+    spread_cot.over_cores()
+    spread_res.finish()
+    turn(res, turned, 0, 16)
     for copy in mid_deltas:
         copy.wait_recv()
-
-    rows = pl.ds(pl.multiple_of(me.dp * 128, 128), 128)
-    for t in range(4):
-        lanes = slice(t * 512, (t + 1) * 512)
-        backs[0, :, lanes] = (
-            dot_nt(mid[1, rows, :], wg[lanes, :]) + dot_nt(mid[2, rows, :], wu[lanes, :])
-        ).astype(BF)
-    backward = collect(backs.at[0], 1)
-    backward.over_x(0)
-    backward.over_x(1)
 
     mid_across.wait_recv()
     spot = mid.at[:, pl.ds(pl.multiple_of(((me.dp + 2) % 4) * 128 + me.y * 32, 32), 32), :]
     mid_far = [send(spot, spot, sem_mid, 6 + k, me.at_y(k)) for k in range(1, me.tall)]
+
+    rows = pl.ds(pl.multiple_of(me.dp * 128, 128), 128)
+    backward = collect(backs.at[0], 1)
+    for low in (1 - me.low, me.low):
+        for h in range(2):
+            lanes = pl.ds(pl.multiple_of(low * 1024 + h * 512, 512), 512)
+            backs[0, :, lanes] = (
+                dot_nt(mid[1, rows, :], wg[lanes, :]) + dot_nt(mid[2, rows, :], wu[lanes, :])
+            ).astype(BF)
+            if low is not me.low:
+                backward.over_x(h)
+    backward.over_z(0)
+    backward.over_z(1)
     for copy in mid_hidden:
         copy.wait_recv()
+    spot = mid.at[:, rows, :]
+    mid_cores = [send(spot, spot, sem_mid, 10, me.sibling())]
     for t in range(2):
         lanes = slice(t * 1024, (t + 1) * 1024)
         backs[1, :, lanes] = dot(mid[0, rows, :], wd[:, lanes]).astype(BF)
-    backward.over_z(0)
-    backward.over_z(1)
     forward = collect(backs.at[1], 2)
     forward.over_x()
-    spread_res.over_cores()
-    spread_cot.over_cores()
 
     held = {}
 
@@ -515,15 +526,6 @@
     for k in range(4):
         work.append(lambda k=k: pick_wide(k))
 
-    for copy in mid_far:
-        copy.wait_recv()
-    mid_cores = []
-    for k, dp in enumerate((me.dp, (me.dp + 2) % 4)):
-        spot = mid.at[:, pl.ds(pl.multiple_of(dp * 128, 128), 128), :]
-        mid_cores.append(send(spot, spot, sem_mid, 10 + k, me.sibling()))
-    spread_res.finish()
-    turn(res, turned, 0, 16)
-
     spread_ig = Spread(me, ig, sem_ig, 2)
     for h in range(2):
         cols = slice(h * 512, (h + 1) * 512)
@@ -531,22 +533,26 @@
         spread_ig.over_z(total.astype(BF), h)
         swap_from[0, :, cols] = total
     swap_ig = swap_out(me, swap_from.at[0], swap_to.at[0], sem_swap, 1)
+    for copy in mid_far:
+        copy.wait_recv()
+    spot = mid.at[:, pl.ds(pl.multiple_of(((me.dp + 2) % 4) * 128, 128), 128), :]
+    mid_cores.append(send(spot, spot, sem_mid, 11, me.sibling()))
+    spread_cot.finish()
     for copy in mid_cores:
         copy.wait_recv()
-    spread_cot.finish()
     fill(1)
-    spread_ig.over_x(fill, 0)
+    spread_ig.over_x(None, 0)
     spread_ig.over_x(None, 1)
     spread_ig.widen()
     forward.over_z()
-    fill(1)
+    fill(2)
 
     rows = spread_ig.group()
     near_sums[me.y] = dot_nt(ig[rows, :], wh[...]).astype(BF)
     spot = near_sums.at[me.y]
     cg_copies = [send(spot, spot, sem_cg, k - 1, me.at_y(k)) for k in range(1, me.tall)]
     spread_ig.forward()
-    fill(2)
+    fill(3)
     spread_ig.over_cores()
 
     swap_from[1] = res[spread_res.chunk(me.z), home].astype(F32) + forward.total()

time: 110 us -> 104 us (0.945)
  the two profiles are of different devices: /device:TPU:2 before, /device:TPU:1 now
where the time goes in v5:
time: 104 us
  Pallas kernels  100 us (96%)
  between operations  3.41 us (3%)
    pallas_call x1, Pallas kernels, chain_call(): pl.pallas_call(chain_kernel, out_shape=shapes, in_specs=[VM] * 11 + [ANY]...  97.8 us
    pallas_call x1, Pallas kernels, finish_call(): pl.pallas_call(finish_kernel, out_shape=[jax.ShapeDtypeStruct(r.shape, BF...  2.44 us

profile of v5, /device:TPU:1, one launch (start us, length us, event | category | flops | bytes accessed | tf_op | source)
XLA Modules:
  0.0 103.6 jit_solution(10446871583683263640)
XLA Ops:
  3.2 97.8 %chain.1 = (bf16[8,2048]{1,0:T(8,128)(2,1)}, bf16[8,2048]{1,0:T(8,128)(2,1)}, bf16[128,256]{1,0:T(8,128)(2,1)}, bf16[60,4096]{1,0:T(8,128)(2,1)}, bf16[60,4096]{...) custom-call(bf16[8,2048]{1,0:T(8,128)(2,1)} %x8.1, bf16[8,2048]{1,0:T(8,128)(2,1)} %cot8.1, ...), custom_call_target="tpu_custom_call" | custom-call | tf_op jit(solution)/shard_map/chain/pallas_call | solution.py:607
  101.0 2.4 %finish.1 = (bf16[8,2048]{1,0:T(8,128)(2,1)}, bf16[8,2048]{1,0:T(8,128)(2,1)}, bf16[128,256]{1,0:T(8,128)(2,1)}, bf16[60,4096]{1,0:T(8,128)(2,1)}, bf16[60,4096]...) custom-call(bf16[8,2048]{1,0:T(8,128)(2,1)} %get-tuple-element.21.refs_0_, ...), custom_call_target="tpu_custom_call" | custom-call | tf_op jit(solution)/shard_map/finish/pallas_call | solution.py:143

commit v6 on v5

--- a/solution.py
+++ b/solution.py
@@ -246,7 +246,7 @@
         at = 16 + h * 8
         self.near.append(self.move(self.chunk(me.z), self.part(h), at, me.beside()))
         for k in sorted(range(1, depth), key=lambda k: min(k, depth - k)):
-            if between is not None and k < depth - k + 1:
+            if between is not None and 2 < k < depth - k + 1:
                 between(1)
             self.first[h][k].wait_recv()
             self.near.append(self.move(self.chunk(me.z + depth - k), self.part(h), at + k, me.beside()))
@@ -541,17 +541,17 @@
     for copy in mid_cores:
         copy.wait_recv()
     fill(1)
-    spread_ig.over_x(None, 0)
+    spread_ig.over_x(fill, 0)
     spread_ig.over_x(None, 1)
     spread_ig.widen()
     forward.over_z()
     fill(2)
 
     rows = spread_ig.group()
+    spread_ig.forward()
     near_sums[me.y] = dot_nt(ig[rows, :], wh[...]).astype(BF)
     spot = near_sums.at[me.y]
     cg_copies = [send(spot, spot, sem_cg, k - 1, me.at_y(k)) for k in range(1, me.tall)]
-    spread_ig.forward()
     fill(3)
     spread_ig.over_cores()
 

time: 104 us -> 103 us (level)
  the two profiles are of different devices: /device:TPU:1 before, /device:TPU:2 now
where the time goes in v6:
time: 103 us; the launch traced here: 101 us
  Pallas kernels  98 us (95%)
  between operations  3.41 us (3%)
    pallas_call x1, Pallas kernels, chain_call(): pl.pallas_call(chain_kernel, out_shape=shapes, in_specs=[VM] * 11 + [ANY]...  95.5 us
    pallas_call x1, Pallas kernels, finish_call(): pl.pallas_call(finish_kernel, out_shape=[jax.ShapeDtypeStruct(r.shape, BF...  2.44 us

profile of v6, /device:TPU:2, one launch (start us, length us, event | category | flops | bytes accessed | tf_op | source)
XLA Modules:
  0.0 101.4 jit_solution(6427735482546720512)
XLA Ops:
  3.2 95.5 %chain.1 = (bf16[8,2048]{1,0:T(8,128)(2,1)}, bf16[8,2048]{1,0:T(8,128)(2,1)}, bf16[128,256]{1,0:T(8,128)(2,1)}, bf16[60,4096]{1,0:T(8,128)(2,1)}, bf16[60,4096]{...) custom-call(bf16[8,2048]{1,0:T(8,128)(2,1)} %x8.1, bf16[8,2048]{1,0:T(8,128)(2,1)} %cot8.1, ...), custom_call_target="tpu_custom_call" | custom-call | tf_op jit(solution)/shard_map/chain/pallas_call | solution.py:607
  98.7 2.4 %finish.1 = (bf16[8,2048]{1,0:T(8,128)(2,1)}, bf16[8,2048]{1,0:T(8,128)(2,1)}, bf16[128,256]{1,0:T(8,128)(2,1)}, bf16[60,4096]{1,0:T(8,128)(2,1)}, bf16[60,4096]...) custom-call(bf16[8,2048]{1,0:T(8,128)(2,1)} %get-tuple-element.21.refs_0_, ...), custom_call_target="tpu_custom_call" | custom-call | tf_op jit(solution)/shard_map/finish/pallas_call | solution.py:143
